TPU v7x, 512 devices: a whole 4x4x16 slice. The times are simulated.
512 devices in a mesh: span: 16 (over y, x), leaf: 32 (over z, core).
Axes of the slice: x: 4, y: 4, z: 16, core: 2. Of those that a mesh axis runs over, the one named last changes fastest.
Arguments:
- populations: float32 [27, 256, 256, 128], P(None, 'span', 'leaf'), may hold values from 0.5 to 1.5
- relax_rates: float32 [27], replicated, may hold values from 1 to 1.6
- marker_forces: float32 [2, 3, 196608], P(None, None, ('span', 'leaf')), may hold values from -6 to 6
- marker_dest: int32 [2, 196608, 1], P(None, ('span', 'leaf')), may hold values from 0 to 31; in each aligned block of 384 rows (0 to 383, 384 to 767, ..., all dimensions but the last counted through in order) at most 36 rows name the same one
- marker_cells: int32 [2, 196608], P(None, ('span', 'leaf')), may hold values from 0 to 16383
Outputs:
- final_state: float32 [27, 256, 256, 128], P(None, 'span', 'leaf')
Inputs may be any that keep to these rules, and one draw needn't show every extreme that they name: `marker_dest`: in each step, no destination is named by more than 36 of the 384 markers of one device, and in every draw some device's markers name one destination exactly 36 times.
All inputs are finite; a program needn't handle non-finite values.
Results may differ from a plain program's by a relative error of at most 0.0001.
Values sent between devices are 32-bit elements; how exact they have to be, the bound alone decides.
No kernel may reach another device: no remote copies, remote signals or barrier semaphores. Data moves between devices by JAX's collectives and lax.ppermute only.
A program may use at most 64 MiB of HBM per device.

v0:
```python
import functools
import jax
import jax.numpy as jnp
import numpy as np
from jax import lax
from jax.experimental import pallas as pl
from jax.experimental.pallas import tpu as pltpu
from jax.sharding import PartitionSpec as P

F32 = jnp.float32
BF16 = jnp.bfloat16
PLANES = 20
WHOLE = pl.BlockSpec(memory_space=pltpu.VMEM)
SCALARS = pl.BlockSpec(memory_space=pltpu.SMEM)
HBM = pl.BlockSpec(memory_space=pl.ANY)


def params(mib):
    return pltpu.CompilerParams(vmem_limit_bytes=mib * 2**20)


def components(q):
    return q // 9 - 1, (q // 3) % 3 - 1, q % 3 - 1


def transform(values, step):
    values = list(values)
    for stride in (9, 3, 1):
        for q in range(27):
            if (q // stride) % 3 == 0:
                triple = (q, q + stride, q + 2 * stride)
                for place, value in zip(triple, step(*[values[i] for i in triple])):
                    values[place] = value
    return values


def to_moments(low, middle, high):
    both = low + high
    return both + middle, high - low, both


def from_moments(zeroth, first, second):
    return second - first, zeroth - second, second + first


def collide(populations, rate, force):
    moments = transform(populations, to_moments)
    density = moments[0]
    momentum = (moments[9], moments[3], moments[1])
    velocity = [part * (1.0 / 27.0) for part in momentum]
    flux = [27.0 * part for part in velocity]
    energy = [3.0 * f * v for f, v in zip(flux, velocity)]
    cross = {}
    for i in range(3):
        for j in range(i + 1, 3):
            cross[i, j] = flux[i] * velocity[j]
    relaxed = []
    for k in range(27):
        powers = (k // 9, (k // 3) % 3, k % 3)
        odd = [i for i in range(3) if powers[i] == 1]
        squares = [i for i in range(3) if powers[i] == 2]
        share = 3.0 ** -len(squares)
        if len(odd) == 0:
            level = density
            for i in squares:
                level = level + energy[i]
        elif len(odd) == 1:
            level = flux[odd[0]]
        elif len(odd) == 2:
            level = cross[odd[0], odd[1]]
        else:
            level = None
        if level is not None and squares:
            level = level * share
        gap = moments[k] if level is None else moments[k] - level
        value = moments[k] - rate(k) * gap
        if force is not None and len(odd) == 1:
            push = force[odd[0]]
            value = value + (push * share if squares else push)
        relaxed.append(value)
    result = transform(relaxed, from_moments)
    scaled = []
    for q in range(27):
        moving = sum(1 for c in components(q) if c != 0)
        scaled.append(result[q] * 0.5**moving if moving else result[q])
    return scaled


def sources(force):
    weight = {1: 2.0 / 9.0, 2: 1.0 / 18.0, 3: 1.0 / 72.0}
    scaled = {n: [part * weight[n] for part in force] for n in weight}
    terms = [None] * 27
    for q in range(14, 27):
        c = components(q)
        total = None
        for i in range(3):
            if c[i] == 0:
                continue
            part = scaled[sum(1 for v in c if v != 0)][i]
            if total is None:
                total = part
            elif c[i] > 0:
                total = total + part
            else:
                total = total - part
        terms[q] = (total, 1)
        terms[26 - q] = (total, -1)
    return terms


def pushed(value, term):
    if term is None:
        return value
    return value + term[0] if term[1] > 0 else value - term[0]


def bin_kernel(forces_ref, dest_ref, cells_ref, sent_ref):
    markers = cells_ref.shape[1]
    leaves = sent_ref.shape[0]
    highest = lax.Precision.HIGHEST
    earlier = (
        lax.broadcasted_iota(jnp.int32, (markers, markers), 0)
        < lax.broadcasted_iota(jnp.int32, (markers, markers), 1)
    ).astype(F32).astype(BF16)
    hot = []
    for t in range(2):
        row = dest_ref[t]
        leaf = lax.broadcasted_iota(jnp.int32, (leaves, markers), 0)
        hot.append((leaf == row).astype(F32))
    ahead = jnp.dot(
        jnp.concatenate(hot, axis=0).astype(BF16), earlier, preferred_element_type=F32
    )
    left, right = [], []
    for t in range(2):
        rank = jnp.sum(hot[t] * ahead[t * leaves : (t + 1) * leaves], axis=0, keepdims=True)
        rank = rank.astype(jnp.int32)
        third = rank // 16
        left.append(jnp.concatenate([jnp.where(third == r, hot[t], 0.0) for r in range(3)], axis=0))
        spot = lax.broadcasted_iota(jnp.int32, (16, markers), 0) == rank % 16
        rows = [cells_ref[t : t + 1, :].astype(F32)] + [forces_ref[c, t : t + 1, :] for c in range(3)]
        own = jnp.concatenate([jnp.where(spot, row, 0.0) for row in rows], axis=0)
        none = jnp.zeros_like(own)
        right.append(jnp.concatenate([own, none] if t == 0 else [none, own], axis=0))
    packed = lax.dot_general(
        jnp.concatenate(left, axis=1),
        jnp.concatenate(right, axis=1),
        (((1,), (1,)), ((), ())),
        precision=highest,
        preferred_element_type=F32,
    )
    for r in range(3):
        sent_ref[:, r, :] = packed[r * leaves : (r + 1) * leaves]


def first_kernel(rates_ref, after_ref, populations_ref, collided_ref):
    width = populations_ref.shape[1]
    base = pl.program_id(0) * width

    def plane(x, carry):
        result = collide(
            [populations_ref[q, x] for q in range(27)], lambda k: rates_ref[k], None
        )
        for q in range(27):
            collided_ref[q, base + x] = result[q]
        return carry

    lax.fori_loop(0, width, plane, 0)


def rows_by_value(received_ref):
    blocks = []
    for r in range(2):
        whole = received_ref[:, r, :]
        blocks += [whole[8 * b : 8 * b + 8] for b in range(4)]
    lane = lax.broadcasted_iota(jnp.int32, (8, 128), 1)
    for half in (4, 2, 1):
        low = (lane // (16 * half)) % 2 == 0
        for b in range(8):
            if b & half:
                continue
            first, second = blocks[b], blocks[b + half]
            blocks[b] = jnp.where(low, first, pltpu.roll(second, 16 * half, 1))
            blocks[b + half] = jnp.where(low, pltpu.roll(first, 128 - 16 * half, 1), second)
    last = received_ref[:, 2, :]
    tail = None
    for b in range(4):
        part = last[8 * b : 8 * b + 8]
        part = jnp.where(lane % 16 < 4, part, 0.0)
        if b:
            part = pltpu.roll(part, 4 * b, 1)
        tail = part if tail is None else tail + part
    sub = lax.broadcasted_iota(jnp.int32, (8, 128), 0)
    rows = []
    for v in range(8):
        spread = pltpu.roll(tail, 128 - 16 * v, 1) if v else tail
        spread = pltpu.roll(spread, 0, 1, stride=16, stride_axis=0)
        spread = jnp.where(lane // 16 == sub, spread, 0.0)
        rows.append((blocks[v], jnp.sum(spread, axis=0, keepdims=True)))
    return rows


def deposit_kernel(parity_ref, received_ref, collided_ref, field_ref, a_ref, b_ref):
    rows = rows_by_value(received_ref)
    index = lax.broadcasted_iota(jnp.int32, (128, 128), 0)
    for t in range(2):
        values = rows[4 * t : 4 * t + 4]
        chunks = [[v[0][s : s + 1] for s in range(8)] + [v[1]] for v in values]
        outer, weighted = [], []
        for s in range(9):
            cell = chunks[0][s].astype(jnp.int32)
            outer.append((index == cell // 128).astype(F32).astype(BF16))
            inner = (index == cell % 128).astype(F32).astype(BF16)
            parts = []
            for c in range(3):
                amount = chunks[c + 1][s]
                big = amount.astype(BF16)
                small = (amount - big.astype(F32)).astype(BF16)
                parts.append((inner * big, inner * small))
            weighted.append(
                jnp.concatenate([p[0] for p in parts] + [p[1] for p in parts], axis=0)
            )
        field = lax.dot_general(
            jnp.concatenate(outer, axis=1),
            jnp.concatenate(weighted, axis=1),
            (((1,), (1,)), ((), ())),
            preferred_element_type=F32,
        )
        for c in range(3):
            whole = field[:, 128 * c : 128 * c + 128] + field[:, 384 + 128 * c : 512 + 128 * c]
            field_ref[t, c] = whole.reshape(field_ref.shape[2:])
    last = collided_ref.shape[1] - 1

    def layers(ref, sign, edge, inside):
        terms = sources([field_ref[0, c, edge] for c in range(3)])
        for n in range(18):
            q = 9 + n if n < 9 else 9 + 9 * sign + n - 9
            ref[n] = pushed(collided_ref[q, edge], terms[q])
        terms = sources([field_ref[0, c, inside] for c in range(3)])
        for n in range(9):
            q = 9 + 9 * sign + n
            ref[18 + n] = pushed(collided_ref[q, inside], terms[q])
        for c in range(3):
            ref[27 + c] = field_ref[1, c, edge]

    @pl.when(parity_ref[0] == 0)
    def _():
        layers(a_ref, 1, last, last - 1)
        layers(b_ref, -1, 0, 1)

    @pl.when(parity_ref[0] != 0)
    def _():
        layers(b_ref, 1, last, last - 1)
        layers(a_ref, -1, 0, 1)


def pack_kernel(parity_ref, collided_ref, field_ref, a_ref, b_ref, halo_ref, up_ref, down_ref):
    @pl.when(parity_ref[0] == 0)
    def _():
        halo_ref[0] = b_ref[...]
        halo_ref[1] = a_ref[...]

    @pl.when(parity_ref[0] != 0)
    def _():
        halo_ref[0] = a_ref[...]
        halo_ref[1] = b_ref[...]

    width = collided_ref.shape[1]
    top = collided_ref.shape[2] - 1
    for ref, sign, edge, inside in ((up_ref, 1, top, top - 1), (down_ref, -1, 0, 1)):
        for ring, z, kinds in ((0, edge, (0, sign)), (1, inside, (sign,))):
            terms = sources([field_ref[0, c, :, z, :] for c in range(3)])
            for order, cz in enumerate(kinds):
                for j in range(9):
                    q = 3 * j + cz + 1
                    place = 18 * ring + 9 * order + j
                    ref[place, pl.ds(2, width), :] = pushed(collided_ref[q, :, z, :], terms[q])
                    cx = j // 3 - 1
                    n = 3 * (j % 3) + cz + 1
                    for side, toward, near, far in ((0, 1, 1, 0), (1, -1, width + 2, width + 3)):
                        if cx == 0:
                            ref[place, pl.ds(near, 1), :] = halo_ref[side, n, pl.ds(z, 1), :]
                        if cx == toward:
                            ref[place, pl.ds(near, 1), :] = halo_ref[side, 9 + n, pl.ds(z, 1), :]
                            ref[place, pl.ds(far, 1), :] = halo_ref[side, 18 + n, pl.ds(z, 1), :]
        for c in range(3):
            ref[27 + c, pl.ds(2, width), :] = field_ref[1, c, :, edge, :]
            ref[27 + c, pl.ds(1, 1), :] = halo_ref[0, 27 + c, pl.ds(edge, 1), :]
            ref[27 + c, pl.ds(width + 2, 1), :] = halo_ref[1, 27 + c, pl.ds(edge, 1), :]


def final_kernel(
    rates_ref, collided_ref, field_ref, halo_ref, up_ref, down_ref, low_ref, high_ref,
    out_ref, state, ring, result, sems,
):
    width, height = collided_ref.shape[1:3]
    sub = lax.broadcasted_iota(jnp.int32, (height, 128), 0)

    def moved(tile, q, low_row, high_row):
        _, cy, cz = components(q)
        if cz > 0:
            tile = jnp.where(sub == 0, low_row(), pltpu.roll(tile, 1, 0))
        elif cz < 0:
            tile = jnp.where(sub == height - 1, high_row(), pltpu.roll(tile, height - 1, 0))
        return pltpu.roll(tile, cy % 128, 1) if cy else tile

    def first_rows(q, row):
        place = 9 + q // 3
        return (
            lambda: low_ref[place, pl.ds(row, 1), :],
            lambda: high_ref[place, pl.ds(row, 1), :],
        )

    def own(x, carry):
        terms = sources([field_ref[0, c, x] for c in range(3)])
        for q in range(27):
            tile = pushed(collided_ref[q, x], terms[q])
            state[q, x + 2 + q // 9 - 1] = moved(tile, q, *first_rows(q, x + 2))
        return carry

    lax.fori_loop(0, width, own, 0)
    for side, toward, near in ((0, 1, 1), (1, -1, width + 2)):
        for n in range(18):
            q = 9 + n if n < 9 else 9 + 9 * toward + n - 9
            tile = halo_ref[side, n]
            state[q, near + q // 9 - 1] = moved(tile, q, *first_rows(q, near))
        for n in range(9):
            q = 9 + 9 * toward + n
            tile = halo_ref[side, 18 + n]
            state[q, near] = moved(tile, q, *first_rows(q, near - toward))

    rate = lambda k: rates_ref[k]
    for side, got, own_sent, toward in ((0, low_ref, down_ref, 1), (1, high_ref, up_ref, -1)):

        def edge(block, carry, side=side, got=got, own_sent=own_sent, toward=toward):
            start = jnp.where(block == 2, 11, 1 + 8 * block)
            values = []
            for q in range(27):
                cx, cy, cz = components(q)
                j = q // 3
                where = pl.ds(start - cx, 8)
                if cz == toward:
                    row = got[18 + j, where, :]
                elif cz == 0:
                    row = got[j, where, :]
                else:
                    row = own_sent[9 + j, where, :]
                values.append(pltpu.roll(row, cy % 128, 1) if cy else row)
            force = [got[27 + c, pl.ds(start, 8), :] for c in range(3)]
            after = collide(values, rate, force)
            for j in range(9):
                ring[side, j, pl.ds(start, 8), :] = after[3 * j + toward + 1]
            return carry

        lax.fori_loop(0, 3, edge, 0)

    def second(x, force):
        after = collide([state[q, x] for q in range(27)], rate, force)
        for q in range(27):
            j = q // 3
            result[q, x + q // 9 - 1] = moved(
                after[q],
                q,
                lambda: ring[0, j, pl.ds(x, 1), :],
                lambda: ring[1, j, pl.ds(x, 1), :],
            )

    second(1, [halo_ref[0, 27 + c] for c in range(3)])
    chunk = 4
    parts = width // chunk

    def copy(part):
        return pltpu.make_async_copy(
            result.at[:, pl.ds(2 + part * chunk, chunk)],
            out_ref.at[:, pl.ds(part * chunk, chunk)],
            sems.at[part],
        )

    def inner(x, carry):
        second(x + 2, [field_ref[1, c, x] for c in range(3)])
        return carry

    done = 0
    for part in range(parts):
        until = min(width, (part + 1) * chunk + 1)
        lax.fori_loop(done, until, inner, 0)
        done = until
        if part == parts - 1:
            second(width + 2, [halo_ref[1, 27 + c] for c in range(3)])
        copy(part).start()
    for part in range(parts):
        copy(part).wait()


def cost(flops, moved):
    return pl.CostEstimate(flops=flops, bytes_accessed=moved, transcendentals=0)


def body(populations, relax_rates, marker_forces, marker_dest, marker_cells):
    width, height, length = populations.shape[1:]
    leaves = lax.axis_size("leaf")
    spans = lax.axis_size("span")
    markers = marker_cells.shape[1]
    held = functools.partial(pltpu.with_memory_space_constraint, memory_space=pltpu.VMEM)
    near = lambda *shape: pltpu.VMEM(shape, F32)
    sent = pl.pallas_call(
        bin_kernel,
        out_shape=near(leaves, 3, 128),
        in_specs=[WHOLE] * 3,
        out_specs=WHOLE,
        compiler_params=params(16),
        name="bin_markers",
    )(
        jnp.transpose(marker_forces, (1, 0, 2)),
        jnp.transpose(marker_dest, (0, 2, 1)),
        marker_cells,
    )
    received = lax.all_to_all(sent, "leaf", 0, 0, tiled=True)
    block = 2
    collided = pl.pallas_call(
        first_kernel,
        grid=(width // block,),
        out_shape=near(*populations.shape),
        in_specs=[
            SCALARS,
            HBM,
            pl.BlockSpec((27, block, height, length), lambda i: (0, i, 0, 0)),
        ],
        out_specs=WHOLE,
        compiler_params=params(16),
        cost_estimate=cost(27 * 12 * width * height * length, 8 * populations.size),
        name="collide_first",
    )(relax_rates, sent, populations)
    parity = lax.rem(lax.axis_index("span"), 2).astype(jnp.int32).reshape(1)
    layer = near(30, height, length)
    field, a_sent, b_sent = pl.pallas_call(
        deposit_kernel,
        out_shape=[near(2, 3, width, height, length), layer, layer],
        in_specs=[SCALARS, WHOLE, WHOLE],
        out_specs=[WHOLE] * 3,
        compiler_params=params(24),
        name="deposit",
    )(parity, held(received), held(collided))
    a_pairs = [(s, s ^ 1) for s in range(spans)]
    b_pairs = [(s, (s + 1 if s % 2 else s - 1) % spans) for s in range(spans)]
    a_got = lax.ppermute(a_sent, "span", a_pairs)
    b_got = lax.ppermute(b_sent, "span", b_pairs)
    face = near(30, 24, length)
    halo, up, down = pl.pallas_call(
        pack_kernel,
        out_shape=[near(2, 30, height, length), face, face],
        in_specs=[SCALARS] + [WHOLE] * 4,
        out_specs=[WHOLE] * 3,
        compiler_params=params(16),
        name="pack_layers",
    )(parity, held(collided), held(field), held(a_got), held(b_got))
    low = lax.ppermute(up, "leaf", [(l, (l + 1) % leaves) for l in range(leaves)])
    high = lax.ppermute(down, "leaf", [(l, (l - 1) % leaves) for l in range(leaves)])
    return pl.pallas_call(
        final_kernel,
        out_shape=jax.ShapeDtypeStruct(populations.shape, F32),
        in_specs=[SCALARS] + [WHOLE] * 7,
        out_specs=HBM,
        scratch_shapes=[
            pltpu.VMEM((27, PLANES, height, length), F32),
            pltpu.VMEM((2, 9, 24, length), F32),
            pltpu.VMEM((27, PLANES, height, length), F32),
            pltpu.SemaphoreType.DMA((width // 4,)),
        ],
        compiler_params=params(32),
        name="collide_second",
    )(relax_rates, held(collided), held(field), held(halo), held(up), held(down), held(low), held(high))


def solution(mesh):
    placed = (
        P(None, "span", "leaf", None),
        P(),
        P(None, None, ("span", "leaf")),
        P(None, ("span", "leaf"), None),
        P(None, ("span", "leaf")),
    )
    return jax.shard_map(
        body, mesh=mesh, in_specs=placed, out_specs=P(None, "span", "leaf", None), check_vma=False
    )
```

profile of v0, /device:TPU:1, one launch (start us, length us, event | category | flops | bytes accessed | tf_op | source)
XLA Modules:
  0.0 64.0 jit_solution(7560894268651122784)
XLA Ops:
  0.0 0.0 copy-start.1
  0.0 0.7 %copy-done.1 = f32[2,3,384]{2,0,1:T(2,128)S(1)} copy-done((f32[2,3,384]{2,0,1:T(2,128)S(1)}, f32[2,3,384]{2,0,1:T(2,128)}, u32[]{:S(2)}) %copy-start.1) | copy-done | bytes 9240
  0.7 0.0 copy-start.2
  0.7 0.7 %copy-done.2 = s32[2,384,1]{1,2,0:T(1,128)S(1)} copy-done((s32[2,384,1]{1,2,0:T(1,128)S(1)}, s32[2,384,1]{1,2,0:T(1,128)}, u32[]{:S(2)}) %copy-start.2) | copy-done | bytes 3096
  1.4 0.7 %copy-done.3 = s32[2,384]{1,0:T(2,128)S(1)} copy-done((s32[2,384]{1,0:T(2,128)S(1)}, s32[2,384]{1,0:T(2,128)}, u32[]{:S(2)}) %copy-start.3) | copy-done | bytes 3096
  2.1 1.3 %bin_markers.1.after_ref = f32[32,3,128]{2,1,0:T(4,128)} custom-call(f32[3,2,384]{2,1,0:T(2,128)S(1)} %bitcast.3, s32[2,1,384]{2,1,0:T(1,128)S(1)} %bitcast.4, s32[2,384]{1,0:T(2,128)S(1)} %copy-done.3), custom_call_target="tpu_custom_call" | custom-call | tf_op jit(solution)/shard_map/bin_markers/pallas_call | solution.py:405
  3.4 16.7 %all-to-all-start = ((f32[32,3,128]{2,1,0:T(4,128)}), f32[32,3,128]{2,1,0:T(4,128)S(1)}, u32[]{:S(2)}, u32[]{:S(2)}) async-start(f32[32,3,128]{2,1,0:T(4,128)} %bin_markers.1.after_ref), calls=%async_computation | async-start | bytes 131072 | tf_op jit(solution)/shard_map/all_to_all | solution.py:417
  20.1 0.0 copy-start
  20.2 1.5 %copy-done = f32[27,16,8,128]{3,2,1,0:T(8,128)S(1)} copy-done((f32[27,16,8,128]{3,2,1,0:T(8,128)S(1)}, f32[27,16,8,128]{3,2,1,0:T(8,128)}, u32[]{:S(2)}) %copy-start) | copy-done | bytes 1769496
  21.6 0.7 %copy-done.4 = f32[27]{0:T(128)S(1)} copy-done((f32[27]{0:T(128)S(1)}, f32[27]{0:T(128)}, u32[]{:S(2)}) %copy-start.4) | copy-done | bytes 132
  22.3 1.7 %collide_first.1.collided_ref = f32[27,16,8,128]{3,2,1,0:T(8,128)S(1)} custom-call(f32[27]{0:T(128)S(1)} %copy-done.4, f32[32,3,128]{2,1,0:T(4,128)} %bin_markers.1.after_ref, f32[27,16,8,128]{3,2,1,0:T(8,128)S(1)} %copy-done), custom_call_target="tpu_custom_call" | custom-call | flops 5308416 | bytes 3538944 | tf_op jit(solution)/shard_map/collide_first/pallas_call | solution.py:419
  24.0 9.3 %all-to-all-done.received_ref = f32[32,3,128]{2,1,0:T(4,128)S(1)} async-done(((f32[32,3,128]{2,1,0:T(4,128)}), f32[32,3,128]{2,1,0:T(4,128)S(1)}, u32[]{:S(2)}, u32[]{:S(2)}) %all-to-all-start) | async-done | bytes 49184 | tf_op jit(solution)/shard_map/all_to_all | solution.py:417
  33.2 1.5 %deposit.1 = (f32[2,3,16,8,128]{4,3,2,1,0:T(8,128)S(1)}, f32[30,8,128]{2,1,0:T(8,128)S(1)}, f32[30,8,128]{2,1,0:T(8,128)S(1)}) custom-call(s32[1]{0:T(128)} %bitcast.2.parity_ref, f32[32,3,128]{2,1,0:T(4,128)S(1)} %all-to-all-done.received_ref, f32[27,16,8,128]{3,2,1,0:T(8,128)S(1)} %collide_first.1.collided_ref), custom_call_target="tpu_custom_call" | custom-call | tf_op jit(solution)/shard_map/deposit/pallas_call | solution.py:435
  34.8 3.1 %collective-permute-start = (f32[30,8,128]{2,1,0:T(8,128)S(1)}, f32[30,8,128]{2,1,0:T(8,128)S(1)}, u32[]{:S(2)}, u32[]{:S(2)}) collective-permute-start(f32[30,8,128]{2,1,0:T(8,128)S(1)} %get-tuple-element.12), channel_id=1, source_target_pairs={{0,32},{32,0},{64,96},{96,64},{128,160},{160,128},{192,224},{224,1... | collective-permute-start | bytes 368648 | tf_op jit(solution)/shard_map/ppermute | solution.py:445
  37.9 6.2 %collective-permute-start.1 = (f32[30,8,128]{2,1,0:T(8,128)S(1)}, f32[30,8,128]{2,1,0:T(8,128)S(1)}, u32[]{:S(2)}, u32[]{:S(2)}) collective-permute-start(f32[30,8,128]{2,1,0:T(8,128)S(1)} %get-tuple-element.13), channel_id=1, source_target_pairs={{0,480},{32,64},{64,32},{96,128},{128,96},{160,192},{192,160},{224... | collective-permute-start | bytes 368648 | tf_op jit(solution)/shard_map/ppermute | solution.py:446
  44.1 0.0 collective-permute-done.a_ref
  44.1 2.8 %collective-permute-done.1.b_ref = f32[30,8,128]{2,1,0:T(8,128)S(1)} collective-permute-done((f32[30,8,128]{2,1,0:T(8,128)S(1)}, f32[30,8,128]{2,1,0:T(8,128)S(1)}, u32[]{:S(2)}, u32[]{:S(2)}) %collective-permute-start.1) | collective-permute-done | bytes 122912 | tf_op jit(solution)/shard_map/ppermute | solution.py:446
  46.8 0.7 %pack_layers.1 = (f32[2,30,8,128]{3,2,1,0:T(8,128)S(1)}, f32[30,24,128]{2,1,0:T(8,128)S(1)}, f32[30,24,128]{2,1,0:T(8,128)S(1)}) custom-call(s32[1]{0:T(128)} %bitcast.2.parity_ref, f32[27,16,8,128]{3,2,1,0:T(8,128)S(1)} %collide_first.1.collided_ref, f32[2,3,16,8,128]{4,3,2,1,0:T(8,128)S(1)} %get-tuple-element.11.field_ref, ...), custom_call_target="tpu_custom_call" | custom-call | tf_op jit(solution)/shard_map/pack_layers/pallas_call | solution.py:448
  47.6 3.2 %collective-permute-start.2 = (f32[30,24,128]{2,1,0:T(8,128)S(1)}, f32[30,24,128]{2,1,0:T(8,128)S(1)}, u32[]{:S(2)}, u32[]{:S(2)}) collective-permute-start(f32[30,24,128]{2,1,0:T(8,128)S(1)} %get-tuple-element.15.up_ref), channel_id=1, source_target_pairs={{0,1},{1,2},{2,3},{3,4},{4,5},{5,6},{6,7},{7,8},{8,9},{9,10},{10,1... | collective-permute-start | bytes 1105928 | tf_op jit(solution)/shard_map/ppermute | solution.py:456
  50.8 0.0 collective-permute-start.3
  50.8 4.5 %collective-permute-done.2.low_ref = f32[30,24,128]{2,1,0:T(8,128)S(1)} collective-permute-done((f32[30,24,128]{2,1,0:T(8,128)S(1)}, f32[30,24,128]{2,1,0:T(8,128)S(1)}, u32[]{:S(2)}, u32[]{:S(2)}) %collective-permute-start.2) | collective-permute-done | bytes 368672 | tf_op jit(solution)/shard_map/ppermute | solution.py:456
  55.2 2.8 %collective-permute-done.3.high_ref = f32[30,24,128]{2,1,0:T(8,128)S(1)} collective-permute-done((f32[30,24,128]{2,1,0:T(8,128)S(1)}, f32[30,24,128]{2,1,0:T(8,128)S(1)}, u32[]{:S(2)}, u32[]{:S(2)}) %collective-permute-start.3) | collective-permute-done | bytes 368672 | tf_op jit(solution)/shard_map/ppermute | solution.py:457
  58.0 0.0 copy-done.5
  58.0 6.0 %collide_second.1 = f32[27,16,8,128]{3,2,1,0:T(8,128)} custom-call(f32[27]{0:T(128)S(1)} %copy-done.5, f32[27,16,8,128]{3,2,1,0:T(8,128)S(1)} %collide_first.1.collided_ref, f32[2,3,16,8,128]{4,3,2,1,0:T(8,128)S(1)} %get-tuple-element.11.field_ref, f32[2,30,8,128]{3,2,1,0:T(8,128)S(1)} %get-tuple-element.14.halo_ref, ...), custom_call_target="tpu_custom_call" | custom-call | tf_op jit(solution)/shard_map/collide_second/pallas_call | solution.py:458
  (3 shorter events, 0.0 us)
Async XLA Ops:
  0.0 0.7 %copy-start.1 = (f32[2,3,384]{2,0,1:T(2,128)S(1)}, f32[2,3,384]{2,0,1:T(2,128)}, u32[]{:S(2)}) copy-start(f32[2,3,384]{2,0,1:T(2,128)} %param.7) | copy-start | bytes 27652
  0.7 0.7 %copy-start.2 = (s32[2,384,1]{1,2,0:T(1,128)S(1)}, s32[2,384,1]{1,2,0:T(1,128)}, u32[]{:S(2)}) copy-start(s32[2,384,1]{1,2,0:T(1,128)} %param.8) | copy-start | bytes 9220
  1.4 0.7 %copy-start.3 = (s32[2,384]{1,0:T(2,128)S(1)}, s32[2,384]{1,0:T(2,128)}, u32[]{:S(2)}) copy-start(s32[2,384]{1,0:T(2,128)} %cells_ref.1) | copy-start | bytes 9220
  3.4 29.8 %all-to-all-start = ((f32[32,3,128]{2,1,0:T(4,128)}), f32[32,3,128]{2,1,0:T(4,128)S(1)}, u32[]{:S(2)}, u32[]{:S(2)}) async-start(f32[32,3,128]{2,1,0:T(4,128)} %bin_markers.1.after_ref), calls=%async_computation | async-start | bytes 131072 | tf_op jit(solution)/shard_map/all_to_all | solution.py:417
  20.1 1.5 %copy-start = (f32[27,16,8,128]{3,2,1,0:T(8,128)S(1)}, f32[27,16,8,128]{3,2,1,0:T(8,128)}, u32[]{:S(2)}) copy-start(f32[27,16,8,128]{3,2,1,0:T(8,128)} %populations_ref.1) | copy-start | bytes 5308420
  21.6 0.7 %copy-start.4 = (f32[27]{0:T(128)S(1)}, f32[27]{0:T(128)}, u32[]{:S(2)}) copy-start(f32[27]{0:T(128)} %rates_ref.3) | copy-start | bytes 328
  33.2 24.8 %copy-start.5 = (f32[27]{0:T(128)S(1)}, f32[27]{0:T(128)}, u32[]{:S(2)}) copy-start(f32[27]{0:T(128)} %rates_ref.3) | copy-start | bytes 328
  34.8 9.3 %collective-permute-start = (f32[30,8,128]{2,1,0:T(8,128)S(1)}, f32[30,8,128]{2,1,0:T(8,128)S(1)}, u32[]{:S(2)}, u32[]{:S(2)}) collective-permute-start(f32[30,8,128]{2,1,0:T(8,128)S(1)} %get-tuple-element.12), channel_id=1, source_target_pairs={{0,32},{32,0},{64,96},{96,64},{128,160},{160,128},{192,224},{224,1... | collective-permute-start | bytes 368648 | tf_op jit(solution)/shard_map/ppermute | solution.py:445
  37.9 8.9 %collective-permute-start.1 = (f32[30,8,128]{2,1,0:T(8,128)S(1)}, f32[30,8,128]{2,1,0:T(8,128)S(1)}, u32[]{:S(2)}, u32[]{:S(2)}) collective-permute-start(f32[30,8,128]{2,1,0:T(8,128)S(1)} %get-tuple-element.13), channel_id=1, source_target_pairs={{0,480},{32,64},{64,32},{96,128},{128,96},{160,192},{192,160},{224... | collective-permute-start | bytes 368648 | tf_op jit(solution)/shard_map/ppermute | solution.py:446
  47.6 7.6 %collective-permute-start.2 = (f32[30,24,128]{2,1,0:T(8,128)S(1)}, f32[30,24,128]{2,1,0:T(8,128)S(1)}, u32[]{:S(2)}, u32[]{:S(2)}) collective-permute-start(f32[30,24,128]{2,1,0:T(8,128)S(1)} %get-tuple-element.15.up_ref), channel_id=1, source_target_pairs={{0,1},{1,2},{2,3},{3,4},{4,5},{5,6},{6,7},{7,8},{8,9},{9,10},{10,1... | collective-permute-start | bytes 1105928 | tf_op jit(solution)/shard_map/ppermute | solution.py:456
  50.8 7.2 %collective-permute-start.3 = (f32[30,24,128]{2,1,0:T(8,128)S(1)}, f32[30,24,128]{2,1,0:T(8,128)S(1)}, u32[]{:S(2)}, u32[]{:S(2)}) collective-permute-start(f32[30,24,128]{2,1,0:T(8,128)S(1)} %get-tuple-element.16.down_ref), channel_id=1, source_target_pairs={{0,31},{1,0},{2,1},{3,2},{4,3},{5,4},{6,5},{7,6},{8,7},{9,8},{10,9... | collective-permute-start | bytes 1105928 | tf_op jit(solution)/shard_map/ppermute | solution.py:457
where the time goes:
time: 64.4 us; the launch traced here: 64 us
  starting transfers between devices  29.2 us (45%)
  waiting for transfers between devices  19.2 us (30%)
  Pallas kernels  11.3 us (18%)
  local copies, waits for them, and re-layouts  4.2 us (7%)
    all_to_all x1, starting transfers between devices, body(): received = lax.all_to_all(sent, 'leaf', 0, 0, tiled=True)  16.7 us
    all_to_all x1, waiting for transfers between devices, body(): received = lax.all_to_all(sent, 'leaf', 0, 0, tiled=True)  9.25 us
    ppermute x1, starting transfers between devices, body(): b_got = lax.ppermute(b_sent, 'span', b_pairs)  6.17 us
    pallas_call x1, Pallas kernels, body(): pl.pallas_call(final_kernel, out_shape=jax.ShapeDtypeStruct(populations.s...  6.05 us
    ppermute x1, waiting for transfers between devices, body(): lax.ppermute(up, 'leaf', [(l, (l + 1) % leaves) for l in range(leaves)])  4.45 us
    unnamed x12, local copies, waits for them, and re-layouts  4.2 us
    ppermute x1, starting transfers between devices, body(): lax.ppermute(up, 'leaf', [(l, (l + 1) % leaves) for l in range(leaves)])  3.19 us
    ppermute x1, starting transfers between devices, body(): a_got = lax.ppermute(a_sent, 'span', a_pairs)  3.12 us
  transfers between devices with their start and end apart: 5, of which 4 were waited for; matrix products, arithmetic and copies ran while one was open for 0% of the time, Pallas kernels for 3%

commit v1 on v0

--- a/solution.py
+++ b/solution.py
@@ -114,9 +114,21 @@
     return value + term[0] if term[1] > 0 else value - term[0]
 
 
-def bin_kernel(forces_ref, dest_ref, cells_ref, sent_ref):
+def group_order(leaves):
+    root = leaves // 2
+    return [root] + [leaf for leaf in range(leaves) if leaf != root]
+
+
+def bin_kernel(forces_hbm, dest_hbm, cells_hbm, sent_ref, forces_ref, dest_ref, cells_ref, sems):
+    pairs = ((dest_hbm, dest_ref), (cells_hbm, cells_ref), (forces_hbm, forces_ref))
+    copies = [pltpu.make_async_copy(a, b, sems.at[i]) for i, (a, b) in enumerate(pairs)]
+    for each in copies:
+        each.start()
+    for each in copies:
+        each.wait()
     markers = cells_ref.shape[1]
     leaves = sent_ref.shape[0]
+    root = leaves // 2
     highest = lax.Precision.HIGHEST
     earlier = (
         lax.broadcasted_iota(jnp.int32, (markers, markers), 0)
@@ -125,6 +137,7 @@
     hot = []
     for t in range(2):
         row = dest_ref[t]
+        row = jnp.where(row < root, row + 1, jnp.where(row == root, 0, row))
         leaf = lax.broadcasted_iota(jnp.int32, (leaves, markers), 0)
         hot.append((leaf == row).astype(F32))
     ahead = jnp.dot(
@@ -288,11 +301,29 @@
             ref[27 + c, pl.ds(width + 2, 1), :] = halo_ref[1, 27 + c, pl.ds(edge, 1), :]
 
 
+def stream_kernel(collided_ref, field_ref, state):
+    width, height = collided_ref.shape[1:3]
+
+    def own(x, carry):
+        terms = sources([field_ref[0, c, x] for c in range(3)])
+        for q in range(27):
+            cx, cy, cz = components(q)
+            tile = pushed(collided_ref[q, x], terms[q])
+            if cz:
+                tile = pltpu.roll(tile, cz % height, 0)
+            if cy:
+                tile = pltpu.roll(tile, cy % 128, 1)
+            state[q, x + 2 + cx] = tile
+        return carry
+
+    lax.fori_loop(0, width, own, 0)
+
+
 def final_kernel(
-    rates_ref, collided_ref, field_ref, halo_ref, up_ref, down_ref, low_ref, high_ref,
+    rates_ref, state_in, field_ref, halo_ref, up_ref, down_ref, low_ref, high_ref,
     out_ref, state, ring, result, sems,
 ):
-    width, height = collided_ref.shape[1:3]
+    width, height = field_ref.shape[2:4]
     sub = lax.broadcasted_iota(jnp.int32, (height, 128), 0)
 
     def moved(tile, q, low_row, high_row):
@@ -310,14 +341,13 @@
             lambda: high_ref[place, pl.ds(row, 1), :],
         )
 
-    def own(x, carry):
-        terms = sources([field_ref[0, c, x] for c in range(3)])
-        for q in range(27):
-            tile = pushed(collided_ref[q, x], terms[q])
-            state[q, x + 2 + q // 9 - 1] = moved(tile, q, *first_rows(q, x + 2))
-        return carry
-
-    lax.fori_loop(0, width, own, 0)
+    for q in range(27):
+        cx, cy, cz = components(q)
+        if cz == 0:
+            continue
+        got, z = (low_ref, 0) if cz > 0 else (high_ref, height - 1)
+        rows = got[9 + q // 3, pl.ds(2, width), :]
+        state[q, pl.ds(2 + cx, width), z, :] = pltpu.roll(rows, cy % 128, 1) if cy else rows
     for side, toward, near in ((0, 1, 1), (1, -1, width + 2)):
         for n in range(18):
             q = 9 + n if n < 9 else 9 + 9 * toward + n - 9
@@ -365,7 +395,7 @@
             )
 
     second(1, [halo_ref[0, 27 + c] for c in range(3)])
-    chunk = 4
+    chunk = 2
     parts = width // chunk
 
     def copy(part):
@@ -401,20 +431,29 @@
     spans = lax.axis_size("span")
     markers = marker_cells.shape[1]
     held = functools.partial(pltpu.with_memory_space_constraint, memory_space=pltpu.VMEM)
+    far = functools.partial(pltpu.with_memory_space_constraint, memory_space=pltpu.HBM)
     near = lambda *shape: pltpu.VMEM(shape, F32)
     sent = pl.pallas_call(
         bin_kernel,
         out_shape=near(leaves, 3, 128),
-        in_specs=[WHOLE] * 3,
+        in_specs=[HBM] * 3,
         out_specs=WHOLE,
+        scratch_shapes=[
+            pltpu.VMEM((3, 2, markers), F32),
+            pltpu.VMEM((2, 1, markers), jnp.int32),
+            pltpu.VMEM((2, markers), jnp.int32),
+            pltpu.SemaphoreType.DMA((3,)),
+        ],
         compiler_params=params(16),
         name="bin_markers",
     )(
-        jnp.transpose(marker_forces, (1, 0, 2)),
-        jnp.transpose(marker_dest, (0, 2, 1)),
-        marker_cells,
+        far(jnp.transpose(marker_forces, (1, 0, 2))),
+        far(jnp.transpose(marker_dest, (0, 2, 1))),
+        far(marker_cells),
     )
-    received = lax.all_to_all(sent, "leaf", 0, 0, tiled=True)
+    received = lax.all_to_all(
+        sent, "leaf", 0, 0, tiled=True, axis_index_groups=[group_order(leaves)]
+    )
     block = 2
     collided = pl.pallas_call(
         first_kernel,
@@ -445,6 +484,16 @@
     a_got = lax.ppermute(a_sent, "span", a_pairs)
     b_got = lax.ppermute(b_sent, "span", b_pairs)
     face = near(30, 24, length)
+    state = near(27, PLANES, height, length)
+    streamed = pl.pallas_call(
+        stream_kernel,
+        out_shape=state,
+        in_specs=[WHOLE] * 2,
+        out_specs=WHOLE,
+        compiler_params=params(16),
+        cost_estimate=cost(27 * 12 * width * height * length, 8 * populations.size),
+        name="stream_first",
+    )(held(collided), held(field))
     halo, up, down = pl.pallas_call(
         pack_kernel,
         out_shape=[near(2, 30, height, length), face, face],
@@ -457,18 +506,18 @@
     high = lax.ppermute(down, "leaf", [(l, (l - 1) % leaves) for l in range(leaves)])
     return pl.pallas_call(
         final_kernel,
-        out_shape=jax.ShapeDtypeStruct(populations.shape, F32),
+        out_shape=[jax.ShapeDtypeStruct(populations.shape, F32), state],
         in_specs=[SCALARS] + [WHOLE] * 7,
-        out_specs=HBM,
+        out_specs=[HBM, WHOLE],
+        input_output_aliases={1: 1},
         scratch_shapes=[
-            pltpu.VMEM((27, PLANES, height, length), F32),
             pltpu.VMEM((2, 9, 24, length), F32),
             pltpu.VMEM((27, PLANES, height, length), F32),
-            pltpu.SemaphoreType.DMA((width // 4,)),
+            pltpu.SemaphoreType.DMA((width // 2,)),
         ],
-        compiler_params=params(32),
+        compiler_params=params(24),
         name="collide_second",
-    )(relax_rates, held(collided), held(field), held(halo), held(up), held(down), held(low), held(high))
+    )(relax_rates, held(streamed), held(field), held(halo), held(up), held(down), held(low), held(high))[0]
 
 
 def solution(mesh):

time: 64.4 us -> 55.8 us (0.87)
  waiting for transfers between devices: 19.2 us -> 8.42 us
  starting transfers between devices: 29.2 us -> 32.6 us
  local copies, waits for them, and re-layouts: 4.2 us -> 2.13 us
  Pallas kernels: 11.3 us -> 12 us
    all_to_all x1, waiting for transfers between devices: 9.25 us -> 0.23 us  [body(): lax.all_to_all(sent, 'leaf', 0, 0, tiled=True, axis_index_groups=[group_o...]
    all_to_all x1, starting transfers between devices: 16.7 us -> 20.1 us  [body(): lax.all_to_all(sent, 'leaf', 0, 0, tiled=True, axis_index_groups=[group_o...]
    unnamed x12 -> x6, local copies, waits for them, and re-layouts: 4.2 us -> 2.13 us
    ppermute x1, waiting for transfers between devices: 4.45 us -> 2.95 us  [body(): lax.ppermute(up, 'leaf', [(l, (l + 1) % leaves) for l in range(leaves)])]
    pallas_call x2 -> x3, Pallas kernels: 7.36 us -> 8.03 us  [the longest x1 4.47 us: body(): pl.pallas_call(final_kernel, out_shape=[jax.ShapeDtypeStruct(populations....]
  transfers between devices with their start and end apart: 5 -> 5, of which waited for: 4 -> 4; matrix products, arithmetic and copies ran while one was open for 0% -> 0% of each run, Pallas kernels for 3% -> 6%
where the time goes in v1:
time: 55.8 us; the launch traced here: 55.2 us
  starting transfers between devices  32.6 us (58%)
  Pallas kernels  12 us (22%)
  waiting for transfers between devices  8.42 us (15%)
  local copies, waits for them, and re-layouts  2.13 us (4%)
    all_to_all x1, starting transfers between devices, body(): lax.all_to_all(sent, 'leaf', 0, 0, tiled=True, axis_index_groups=[group_o...  20.1 us
    ppermute x1, starting transfers between devices, body(): b_got = lax.ppermute(b_sent, 'span', b_pairs)  6.17 us
    pallas_call x1, Pallas kernels, body(): pl.pallas_call(final_kernel, out_shape=[jax.ShapeDtypeStruct(populations....  4.47 us
    ppermute x1, starting transfers between devices, body(): a_got = lax.ppermute(a_sent, 'span', a_pairs)  3.13 us
    ppermute x1, starting transfers between devices, body(): lax.ppermute(up, 'leaf', [(l, (l + 1) % leaves) for l in range(leaves)])  3.11 us
    ppermute x1, waiting for transfers between devices, body(): lax.ppermute(up, 'leaf', [(l, (l + 1) % leaves) for l in range(leaves)])  2.95 us
    ppermute x1, waiting for transfers between devices, body(): b_got = lax.ppermute(b_sent, 'span', b_pairs)  2.75 us
    ppermute x1, waiting for transfers between devices, body(): lax.ppermute(down, 'leaf', [(l, (l - 1) % leaves) for l in range(leaves)])  2.48 us
  transfers between devices with their start and end apart: 5, of which 4 were waited for; matrix products, arithmetic and copies ran while one was open for 0% of the time, Pallas kernels for 6%

profile of v1, /device:TPU:1, one launch (start us, length us, event | category | flops | bytes accessed | tf_op | source)
XLA Modules:
  0.0 55.2 jit_solution(340305134332673482)
XLA Ops:
  0.0 2.1 %bin_markers.1.after_ref = f32[32,3,128]{2,1,0:T(4,128)} custom-call(f32[3,2,384]{2,1,0:T(2,128)} %bitcast.3, s32[2,1,384]{2,1,0:T(1,128)} %bitcast.4, s32[2,384]{1,0:T(2,128)} %cells_hbm.1), custom_call_target="tpu_custom_call" | custom-call | tf_op jit(solution)/shard_map/bin_markers/pallas_call | solution.py:436
  2.1 20.1 %all-to-all-start = ((f32[32,3,128]{2,1,0:T(4,128)}), f32[32,3,128]{2,1,0:T(4,128)S(1)}, u32[]{:S(2)}, u32[]{:S(2)}) async-start(f32[32,3,128]{2,1,0:T(4,128)} %bin_markers.1.after_ref), calls=%async_computation | async-start | bytes 131072 | tf_op jit(solution)/shard_map/all_to_all | solution.py:454
  22.2 0.0 copy-start
  22.2 1.5 %copy-done = f32[27,16,8,128]{3,2,1,0:T(8,128)S(1)} copy-done((f32[27,16,8,128]{3,2,1,0:T(8,128)S(1)}, f32[27,16,8,128]{3,2,1,0:T(8,128)}, u32[]{:S(2)}) %copy-start) | copy-done | bytes 1769496
  23.7 0.0 copy-start.1
  23.7 0.7 %copy-done.1 = f32[27]{0:T(128)S(1)} copy-done((f32[27]{0:T(128)S(1)}, f32[27]{0:T(128)}, u32[]{:S(2)}) %copy-start.1) | copy-done | bytes 132
  24.4 1.7 %collide_first.1.collided_ref = f32[27,16,8,128]{3,2,1,0:T(8,128)S(1)} custom-call(f32[27]{0:T(128)S(1)} %copy-done.1, f32[32,3,128]{2,1,0:T(4,128)} %bin_markers.1.after_ref, f32[27,16,8,128]{3,2,1,0:T(8,128)S(1)} %copy-done), custom_call_target="tpu_custom_call" | custom-call | flops 5308416 | bytes 3538944 | tf_op jit(solution)/shard_map/collide_first/pallas_call | solution.py:458
  26.0 0.2 all-to-all-done.received_ref
  26.3 1.5 %deposit.1 = (f32[2,3,16,8,128]{4,3,2,1,0:T(8,128)S(1)}, f32[30,8,128]{2,1,0:T(8,128)S(1)}, f32[30,8,128]{2,1,0:T(8,128)S(1)}) custom-call(s32[1]{0:T(128)} %bitcast.2.parity_ref, f32[32,3,128]{2,1,0:T(4,128)S(1)} %all-to-all-done.received_ref, f32[27,16,8,128]{3,2,1,0:T(8,128)S(1)} %collide_first.1.collided_ref), custom_call_target="tpu_custom_call" | custom-call | tf_op jit(solution)/shard_map/deposit/pallas_call | solution.py:474
  27.8 3.1 %collective-permute-start = (f32[30,8,128]{2,1,0:T(8,128)S(1)}, f32[30,8,128]{2,1,0:T(8,128)S(1)}, u32[]{:S(2)}, u32[]{:S(2)}) collective-permute-start(f32[30,8,128]{2,1,0:T(8,128)S(1)} %get-tuple-element.13), channel_id=1, source_target_pairs={{0,32},{32,0},{64,96},{96,64},{128,160},{160,128},{192,224},{224,1... | collective-permute-start | bytes 368648 | tf_op jit(solution)/shard_map/ppermute | solution.py:484
  31.0 6.2 %collective-permute-start.1 = (f32[30,8,128]{2,1,0:T(8,128)S(1)}, f32[30,8,128]{2,1,0:T(8,128)S(1)}, u32[]{:S(2)}, u32[]{:S(2)}) collective-permute-start(f32[30,8,128]{2,1,0:T(8,128)S(1)} %get-tuple-element.14), channel_id=1, source_target_pairs={{0,480},{32,64},{64,32},{96,128},{128,96},{160,192},{192,160},{224... | collective-permute-start | bytes 368648 | tf_op jit(solution)/shard_map/ppermute | solution.py:485
  37.1 0.0 collective-permute-done.a_ref
  37.2 2.8 %collective-permute-done.1.b_ref = f32[30,8,128]{2,1,0:T(8,128)S(1)} collective-permute-done((f32[30,8,128]{2,1,0:T(8,128)S(1)}, f32[30,8,128]{2,1,0:T(8,128)S(1)}, u32[]{:S(2)}, u32[]{:S(2)}) %collective-permute-start.1) | collective-permute-done | bytes 122912 | tf_op jit(solution)/shard_map/ppermute | solution.py:485
  39.9 0.7 %pack_layers.1 = (f32[2,30,8,128]{3,2,1,0:T(8,128)S(1)}, f32[30,24,128]{2,1,0:T(8,128)S(1)}, f32[30,24,128]{2,1,0:T(8,128)S(1)}) custom-call(s32[1]{0:T(128)} %bitcast.2.parity_ref, f32[27,16,8,128]{3,2,1,0:T(8,128)S(1)} %collide_first.1.collided_ref, f32[2,3,16,8,128]{4,3,2,1,0:T(8,128)S(1)} %get-tuple-element.12.field_ref, ...), custom_call_target="tpu_custom_call" | custom-call | tf_op jit(solution)/shard_map/pack_layers/pallas_call | solution.py:497
  40.6 3.1 %collective-permute-start.2 = (f32[30,24,128]{2,1,0:T(8,128)S(1)}, f32[30,24,128]{2,1,0:T(8,128)S(1)}, u32[]{:S(2)}, u32[]{:S(2)}) collective-permute-start(f32[30,24,128]{2,1,0:T(8,128)S(1)} %get-tuple-element.16.up_ref), channel_id=1, source_target_pairs={{0,1},{1,2},{2,3},{3,4},{4,5},{5,6},{6,7},{7,8},{8,9},{9,10},{10,1... | collective-permute-start | bytes 1105928 | tf_op jit(solution)/shard_map/ppermute | solution.py:505
  43.8 0.0 copy-start.2
  43.8 0.0 collective-permute-start.3
  43.8 1.5 %stream_first.1.state_in = f32[27,20,8,128]{3,2,1,0:T(8,128)S(1)} custom-call(f32[27,16,8,128]{3,2,1,0:T(8,128)S(1)} %collide_first.1.collided_ref, f32[2,3,16,8,128]{4,3,2,1,0:T(8,128)S(1)} %get-tuple-element.12.field_ref), custom_call_target="tpu_custom_call" | custom-call | flops 5308416 | bytes 3538944 | tf_op jit(solution)/shard_map/stream_first/pallas_call | solution.py:488
  45.3 2.9 %collective-permute-done.2.low_ref = f32[30,24,128]{2,1,0:T(8,128)S(1)} collective-permute-done((f32[30,24,128]{2,1,0:T(8,128)S(1)}, f32[30,24,128]{2,1,0:T(8,128)S(1)}, u32[]{:S(2)}, u32[]{:S(2)}) %collective-permute-start.2) | collective-permute-done | bytes 368672 | tf_op jit(solution)/shard_map/ppermute | solution.py:505
  48.2 2.5 %collective-permute-done.3.high_ref = f32[30,24,128]{2,1,0:T(8,128)S(1)} collective-permute-done((f32[30,24,128]{2,1,0:T(8,128)S(1)}, f32[30,24,128]{2,1,0:T(8,128)S(1)}, u32[]{:S(2)}, u32[]{:S(2)}) %collective-permute-start.3) | collective-permute-done | bytes 368672 | tf_op jit(solution)/shard_map/ppermute | solution.py:506
  50.7 0.0 copy-done.2
  50.7 4.5 %collide_second.1 = (f32[27,16,8,128]{3,2,1,0:T(8,128)}, f32[27,20,8,128]{3,2,1,0:T(8,128)S(1)}) custom-call(f32[27]{0:T(128)S(1)} %copy-done.2, f32[27,20,8,128]{3,2,1,0:T(8,128)S(1)} %stream_first.1.state_in, f32[2,3,16,8,128]{4,3,2,1,0:T(8,128)S(1)} %get-tuple-element.12.field_ref, ...), custom_call_target="tpu_custom_call", output_to_operand_aliasing={{1}: (1, {})} | custom-call | tf_op jit(solution)/shard_map/collide_second/pallas_call | solution.py:507
Async XLA Ops:
  2.1 24.2 %all-to-all-start = ((f32[32,3,128]{2,1,0:T(4,128)}), f32[32,3,128]{2,1,0:T(4,128)S(1)}, u32[]{:S(2)}, u32[]{:S(2)}) async-start(f32[32,3,128]{2,1,0:T(4,128)} %bin_markers.1.after_ref), calls=%async_computation | async-start | bytes 131072 | tf_op jit(solution)/shard_map/all_to_all | solution.py:454
  22.2 1.5 %copy-start = (f32[27,16,8,128]{3,2,1,0:T(8,128)S(1)}, f32[27,16,8,128]{3,2,1,0:T(8,128)}, u32[]{:S(2)}) copy-start(f32[27,16,8,128]{3,2,1,0:T(8,128)} %populations_ref.1) | copy-start | bytes 5308420
  23.7 0.7 %copy-start.1 = (f32[27]{0:T(128)S(1)}, f32[27]{0:T(128)}, u32[]{:S(2)}) copy-start(f32[27]{0:T(128)} %rates_ref.3) | copy-start | bytes 328
  27.8 9.3 %collective-permute-start = (f32[30,8,128]{2,1,0:T(8,128)S(1)}, f32[30,8,128]{2,1,0:T(8,128)S(1)}, u32[]{:S(2)}, u32[]{:S(2)}) collective-permute-start(f32[30,8,128]{2,1,0:T(8,128)S(1)} %get-tuple-element.13), channel_id=1, source_target_pairs={{0,32},{32,0},{64,96},{96,64},{128,160},{160,128},{192,224},{224,1... | collective-permute-start | bytes 368648 | tf_op jit(solution)/shard_map/ppermute | solution.py:484
  31.0 8.9 %collective-permute-start.1 = (f32[30,8,128]{2,1,0:T(8,128)S(1)}, f32[30,8,128]{2,1,0:T(8,128)S(1)}, u32[]{:S(2)}, u32[]{:S(2)}) collective-permute-start(f32[30,8,128]{2,1,0:T(8,128)S(1)} %get-tuple-element.14), channel_id=1, source_target_pairs={{0,480},{32,64},{64,32},{96,128},{128,96},{160,192},{192,160},{224... | collective-permute-start | bytes 368648 | tf_op jit(solution)/shard_map/ppermute | solution.py:485
  40.6 7.6 %collective-permute-start.2 = (f32[30,24,128]{2,1,0:T(8,128)S(1)}, f32[30,24,128]{2,1,0:T(8,128)S(1)}, u32[]{:S(2)}, u32[]{:S(2)}) collective-permute-start(f32[30,24,128]{2,1,0:T(8,128)S(1)} %get-tuple-element.16.up_ref), channel_id=1, source_target_pairs={{0,1},{1,2},{2,3},{3,4},{4,5},{5,6},{6,7},{7,8},{8,9},{9,10},{10,1... | collective-permute-start | bytes 1105928 | tf_op jit(solution)/shard_map/ppermute | solution.py:505
  43.8 6.9 %copy-start.2 = (f32[27]{0:T(128)S(1)}, f32[27]{0:T(128)}, u32[]{:S(2)}) copy-start(f32[27]{0:T(128)} %rates_ref.3) | copy-start | bytes 328
  43.8 6.9 %collective-permute-start.3 = (f32[30,24,128]{2,1,0:T(8,128)S(1)}, f32[30,24,128]{2,1,0:T(8,128)S(1)}, u32[]{:S(2)}, u32[]{:S(2)}) collective-permute-start(f32[30,24,128]{2,1,0:T(8,128)S(1)} %get-tuple-element.17.down_ref), channel_id=1, source_target_pairs={{0,31},{1,0},{2,1},{3,2},{4,3},{5,4},{6,5},{7,6},{8,7},{9,8},{10,9... | collective-permute-start | bytes 1105928 | tf_op jit(solution)/shard_map/ppermute | solution.py:506

commit v2 on v0

--- a/solution.py
+++ b/solution.py
@@ -9,6 +9,7 @@
 
 F32 = jnp.float32
 BF16 = jnp.bfloat16
+SPLIT = 7
 PLANES = 20
 WHOLE = pl.BlockSpec(memory_space=pltpu.VMEM)
 SCALARS = pl.BlockSpec(memory_space=pltpu.SMEM)
@@ -114,22 +115,36 @@
     return value + term[0] if term[1] > 0 else value - term[0]
 
 
-def bin_kernel(forces_ref, dest_ref, cells_ref, sent_ref):
+def group_order(leaves):
+    root = leaves * 5 // 8
+    return [root] + [leaf for leaf in range(leaves) if leaf != root]
+
+
+def bin_kernel(forces_hbm, dest_hbm, cells_hbm, sent_ref, forces_ref, dest_ref, cells_ref, sems):
+    pairs = ((dest_hbm, dest_ref), (cells_hbm, cells_ref), (forces_hbm, forces_ref))
+    copies = [pltpu.make_async_copy(a, b, sems.at[i]) for i, (a, b) in enumerate(pairs)]
+    for each in copies:
+        each.start()
     markers = cells_ref.shape[1]
     leaves = sent_ref.shape[0]
+    root = leaves * 5 // 8
     highest = lax.Precision.HIGHEST
     earlier = (
         lax.broadcasted_iota(jnp.int32, (markers, markers), 0)
         < lax.broadcasted_iota(jnp.int32, (markers, markers), 1)
     ).astype(F32).astype(BF16)
+    copies[0].wait()
     hot = []
     for t in range(2):
         row = dest_ref[t]
+        row = jnp.where(row < root, row + 1, jnp.where(row == root, 0, row))
         leaf = lax.broadcasted_iota(jnp.int32, (leaves, markers), 0)
         hot.append((leaf == row).astype(F32))
     ahead = jnp.dot(
         jnp.concatenate(hot, axis=0).astype(BF16), earlier, preferred_element_type=F32
     )
+    copies[1].wait()
+    copies[2].wait()
     left, right = [], []
     for t in range(2):
         rank = jnp.sum(hot[t] * ahead[t * leaves : (t + 1) * leaves], axis=0, keepdims=True)
@@ -199,23 +214,44 @@
     return rows
 
 
-def deposit_kernel(parity_ref, received_ref, collided_ref, field_ref, a_ref, b_ref):
+def rows_of(height, sign):
+    edge, inside = (height - 1, height - 2) if sign > 0 else (0, 1)
+    return ((edge, 0, (0, sign)), (inside, 18, (sign,)))
+
+
+def own_faces(collided_ref, field_ref, up_ref, down_ref):
+    height = collided_ref.shape[2]
+    for ref, sign in ((up_ref, 1), (down_ref, -1)):
+        for z, first, kinds in rows_of(height, sign):
+            terms = sources([field_ref[0, c, :, z, :] for c in range(3)])
+            for order, cz in enumerate(kinds):
+                for j in range(9):
+                    q = 3 * j + cz + 1
+                    ref[first + 9 * order + j] = pushed(collided_ref[q, :, z, :], terms[q])
+        for c in range(3):
+            ref[27 + c] = field_ref[1, c, :, height - 1 if sign > 0 else 0, :]
+
+
+def deposit_kernel(
+    parity_ref, received_ref, collided_ref, field_ref, a_ref, b_ref, up_ref, down_ref
+):
     rows = rows_by_value(received_ref)
-    index = lax.broadcasted_iota(jnp.int32, (128, 128), 0)
+    index = lax.broadcasted_iota(jnp.int32, (128, 128), 0).astype(F32).astype(BF16)
+    one, zero = jnp.ones((), BF16), jnp.zeros((), BF16)
     for t in range(2):
         values = rows[4 * t : 4 * t + 4]
         chunks = [[v[0][s : s + 1] for s in range(8)] + [v[1]] for v in values]
         outer, weighted = [], []
         for s in range(9):
             cell = chunks[0][s].astype(jnp.int32)
-            outer.append((index == cell // 128).astype(F32).astype(BF16))
-            inner = (index == cell % 128).astype(F32).astype(BF16)
+            outer.append(jnp.where(index == (cell // 128).astype(F32).astype(BF16), one, zero))
+            inner = index == (cell % 128).astype(F32).astype(BF16)
             parts = []
             for c in range(3):
                 amount = chunks[c + 1][s]
                 big = amount.astype(BF16)
                 small = (amount - big.astype(F32)).astype(BF16)
-                parts.append((inner * big, inner * small))
+                parts.append((jnp.where(inner, big, zero), jnp.where(inner, small, zero)))
             weighted.append(
                 jnp.concatenate([p[0] for p in parts] + [p[1] for p in parts], axis=0)
             )
@@ -252,8 +288,14 @@
         layers(b_ref, 1, last, last - 1)
         layers(a_ref, -1, 0, 1)
 
-
-def pack_kernel(parity_ref, collided_ref, field_ref, a_ref, b_ref, halo_ref, up_ref, down_ref):
+    own_faces(collided_ref, field_ref, up_ref, down_ref)
+
+
+def corner_at(place, number):
+    return place // 2, pl.ds(4 * (place % 2) + number, 1)
+
+
+def corner_kernel(parity_ref, a_ref, b_ref, after_ref, halo_ref, up_ref, down_ref):
     @pl.when(parity_ref[0] == 0)
     def _():
         halo_ref[0] = b_ref[...]
@@ -264,131 +306,203 @@
         halo_ref[0] = a_ref[...]
         halo_ref[1] = b_ref[...]
 
-    width = collided_ref.shape[1]
-    top = collided_ref.shape[2] - 1
-    for ref, sign, edge, inside in ((up_ref, 1, top, top - 1), (down_ref, -1, 0, 1)):
-        for ring, z, kinds in ((0, edge, (0, sign)), (1, inside, (sign,))):
-            terms = sources([field_ref[0, c, :, z, :] for c in range(3)])
+    height = a_ref.shape[1]
+    for ref, sign in ((up_ref, 1), (down_ref, -1)):
+
+        def put(place, number, side, layer, z):
+            tile, row = corner_at(place, number)
+            ref[tile, row, :] = halo_ref[side, layer, pl.ds(z, 1), :]
+
+        for z, first, kinds in rows_of(height, sign):
             for order, cz in enumerate(kinds):
                 for j in range(9):
-                    q = 3 * j + cz + 1
-                    place = 18 * ring + 9 * order + j
-                    ref[place, pl.ds(2, width), :] = pushed(collided_ref[q, :, z, :], terms[q])
+                    place = first + 9 * order + j
                     cx = j // 3 - 1
                     n = 3 * (j % 3) + cz + 1
-                    for side, toward, near, far in ((0, 1, 1, 0), (1, -1, width + 2, width + 3)):
+                    for side, toward, near, far in ((0, 1, 1, 0), (1, -1, 2, 3)):
                         if cx == 0:
-                            ref[place, pl.ds(near, 1), :] = halo_ref[side, n, pl.ds(z, 1), :]
+                            put(place, near, side, n, z)
                         if cx == toward:
-                            ref[place, pl.ds(near, 1), :] = halo_ref[side, 9 + n, pl.ds(z, 1), :]
-                            ref[place, pl.ds(far, 1), :] = halo_ref[side, 18 + n, pl.ds(z, 1), :]
+                            put(place, near, side, 9 + n, z)
+                            put(place, far, side, 18 + n, z)
+        edge = height - 1 if sign > 0 else 0
         for c in range(3):
-            ref[27 + c, pl.ds(2, width), :] = field_ref[1, c, :, edge, :]
-            ref[27 + c, pl.ds(1, 1), :] = halo_ref[0, 27 + c, pl.ds(edge, 1), :]
-            ref[27 + c, pl.ds(width + 2, 1), :] = halo_ref[1, 27 + c, pl.ds(edge, 1), :]
-
-
-def final_kernel(
-    rates_ref, collided_ref, field_ref, halo_ref, up_ref, down_ref, low_ref, high_ref,
-    out_ref, state, ring, result, sems,
-):
-    width, height = collided_ref.shape[1:3]
-    sub = lax.broadcasted_iota(jnp.int32, (height, 128), 0)
-
-    def moved(tile, q, low_row, high_row):
-        _, cy, cz = components(q)
+            put(27 + c, 1, 0, 27 + c, edge)
+            put(27 + c, 2, 1, 27 + c, edge)
+
+
+def moved(tile, q, low_row, high_row):
+    _, cy, cz = components(q)
+    height = tile.shape[0]
+    if cz:
+        sub = lax.broadcasted_iota(jnp.int32, tile.shape, 0)
         if cz > 0:
             tile = jnp.where(sub == 0, low_row(), pltpu.roll(tile, 1, 0))
-        elif cz < 0:
+        else:
             tile = jnp.where(sub == height - 1, high_row(), pltpu.roll(tile, height - 1, 0))
-        return pltpu.roll(tile, cy % 128, 1) if cy else tile
-
-    def first_rows(q, row):
-        place = 9 + q // 3
-        return (
-            lambda: low_ref[place, pl.ds(row, 1), :],
-            lambda: high_ref[place, pl.ds(row, 1), :],
+    return pltpu.roll(tile, cy % 128, 1) if cy else tile
+
+
+def edge_rows(got, sent, toward, start, force, rate):
+    values = []
+    for q in range(27):
+        cx, cy, cz = components(q)
+        j = q // 3
+        where = pl.ds(start - cx, 8)
+        if cz == toward:
+            row = got(18 + j, where)
+        elif cz == 0:
+            row = got(j, where)
+        else:
+            row = sent(9 + j, where)
+        values.append(pltpu.roll(row, cy % 128, 1) if cy else row)
+    after = collide(values, rate, force)
+    return [after[3 * j + toward + 1] for j in range(9)]
+
+
+def second(x, force, rate, state, ring, result):
+    after = collide([state[q, x] for q in range(27)], rate, force)
+    for q in range(27):
+        j = q // 3
+        result[q, x + q // 9 - 1] = moved(
+            after[q],
+            q,
+            lambda: ring[0, j, pl.ds(x, 1), :],
+            lambda: ring[1, j, pl.ds(x, 1), :],
         )
+
+
+def write_out(result, out_ref, sem, plane, count):
+    return pltpu.make_async_copy(
+        result.at[:, pl.ds(2 + plane, count)], out_ref.at[:, pl.ds(plane, count)], sem
+    )
+
+
+def planes(first, last, rate, field_ref, state, ring, result, out_ref, sems):
+    def plane(x, carry):
+        second(x + 2, [field_ref[1, c, x] for c in range(3)], rate, state, ring, result)
+        return carry
+
+    copies = []
+    done = first
+    for place in range(max(2, first - 1), last - 2, 2):
+        lax.fori_loop(done, place + 3, plane, 0)
+        done = place + 3
+        copies.append(write_out(result, out_ref, sems.at[len(copies)], place, 2))
+        copies[-1].start()
+    for each in copies:
+        each.wait()
+
+
+def inner_kernel(
+    rates_ref, collided_ref, field_ref, up_ref, down_ref, low_ref, high_ref,
+    out_ref, state, result, ring, sems,
+):
+    width = collided_ref.shape[1]
+    rate = lambda k: rates_ref[k]
 
     def own(x, carry):
         terms = sources([field_ref[0, c, x] for c in range(3)])
         for q in range(27):
+            place = 9 + q // 3
             tile = pushed(collided_ref[q, x], terms[q])
-            state[q, x + 2 + q // 9 - 1] = moved(tile, q, *first_rows(q, x + 2))
+            state[q, x + 2 + q // 9 - 1] = moved(
+                tile,
+                q,
+                lambda: low_ref[place, pl.ds(x, 1), :],
+                lambda: high_ref[place, pl.ds(x, 1), :],
+            )
         return carry
 
     lax.fori_loop(0, width, own, 0)
+    for side, got, sent, toward in ((0, low_ref, down_ref, 1), (1, high_ref, up_ref, -1)):
+
+        def edge(block, carry, side=side, got=got, sent=sent, toward=toward):
+            start = 1 + (width - 10) * block
+            force = [got[27 + c, pl.ds(start, 8), :] for c in range(3)]
+            rows = edge_rows(
+                lambda place, where: got[place, where, :],
+                lambda place, where: sent[place, where, :],
+                toward, start, force, rate,
+            )
+            for j in range(9):
+                ring[side, j, pl.ds(start + 2, 8), :] = rows[j]
+            return carry
+
+        lax.fori_loop(0, 2, edge, 0)
+    planes(1, SPLIT, rate, field_ref, state, ring, result, out_ref, sems)
+
+
+def more_kernel(
+    rates_ref, state, field_ref, ring, result_in, out_in, out_ref, result, sems
+):
+    width = field_ref.shape[2]
+    rate = lambda k: rates_ref[k]
+    planes(SPLIT, width - 1, rate, field_ref, state, ring, result, out_ref, sems)
+
+
+def outer_kernel(
+    rates_ref, halo_ref, state_in, result_in, out_in, field_ref,
+    up_ref, down_ref, low_ref, high_ref,
+    up_corner, down_corner, low_corner, high_corner,
+    out_ref, state, result, got, sent, ring, sems,
+):
+    width = field_ref.shape[2]
+    rate = lambda k: rates_ref[k]
+    columns = (0, 1, width + 2, width + 3)
     for side, toward, near in ((0, 1, 1), (1, -1, width + 2)):
-        for n in range(18):
-            q = 9 + n if n < 9 else 9 + 9 * toward + n - 9
-            tile = halo_ref[side, n]
-            state[q, near + q // 9 - 1] = moved(tile, q, *first_rows(q, near))
-        for n in range(9):
-            q = 9 + 9 * toward + n
-            tile = halo_ref[side, 18 + n]
-            state[q, near] = moved(tile, q, *first_rows(q, near - toward))
-
-    rate = lambda k: rates_ref[k]
-    for side, got, own_sent, toward in ((0, low_ref, down_ref, 1), (1, high_ref, up_ref, -1)):
-
-        def edge(block, carry, side=side, got=got, own_sent=own_sent, toward=toward):
-            start = jnp.where(block == 2, 11, 1 + 8 * block)
-            values = []
-            for q in range(27):
-                cx, cy, cz = components(q)
-                j = q // 3
-                where = pl.ds(start - cx, 8)
-                if cz == toward:
-                    row = got[18 + j, where, :]
-                elif cz == 0:
-                    row = got[j, where, :]
-                else:
-                    row = own_sent[9 + j, where, :]
-                values.append(pltpu.roll(row, cy % 128, 1) if cy else row)
-            force = [got[27 + c, pl.ds(start, 8), :] for c in range(3)]
-            after = collide(values, rate, force)
+        for n in range(27):
+            q = 9 + n if n < 9 else 9 + 9 * toward + n % 9
+            column = near if n < 18 else near - toward
+            place = 9 + q // 3
+            tile, row = corner_at(place, columns.index(column))
+            state[q, column + q // 9 - 1] = moved(
+                halo_ref[side, n],
+                q,
+                lambda: low_corner[tile, row, :],
+                lambda: high_corner[tile, row, :],
+            )
+
+    def gather(target, place, own, corner, source):
+        target[place, pl.ds(2, width), :] = own[source]
+        for number, column in enumerate(columns):
+            tile, row = corner_at(source, number)
+            target[place, pl.ds(column, 1), :] = corner[tile, row, :]
+
+    sides = (
+        (0, low_ref, low_corner, down_ref, down_corner, 1),
+        (1, high_ref, high_corner, up_ref, up_corner, -1),
+    )
+    for side, mine, corner, left, left_corner, toward in sides:
+        for place in list(range(9)) + list(range(18, 30)):
+            gather(got.at[side], place, mine, corner, place)
+        for j in range(9):
+            gather(sent.at[side], j, left, left_corner, 9 + j)
+
+        def edge(block, carry, side=side, toward=toward):
+            start = 1 + (width - 6) * block
+            force = [got[side, 27 + c, pl.ds(start, 8), :] for c in range(3)]
+            rows = edge_rows(
+                lambda place, where: got[side, place, where, :],
+                lambda place, where: sent[side, place - 9, where, :],
+                toward, start, force, rate,
+            )
             for j in range(9):
-                ring[side, j, pl.ds(start, 8), :] = after[3 * j + toward + 1]
+                ring[side, j, pl.ds(start, 8), :] = rows[j]
             return carry
 
-        lax.fori_loop(0, 3, edge, 0)
-
-    def second(x, force):
-        after = collide([state[q, x] for q in range(27)], rate, force)
-        for q in range(27):
-            j = q // 3
-            result[q, x + q // 9 - 1] = moved(
-                after[q],
-                q,
-                lambda: ring[0, j, pl.ds(x, 1), :],
-                lambda: ring[1, j, pl.ds(x, 1), :],
-            )
-
-    second(1, [halo_ref[0, 27 + c] for c in range(3)])
-    chunk = 4
-    parts = width // chunk
-
-    def copy(part):
-        return pltpu.make_async_copy(
-            result.at[:, pl.ds(2 + part * chunk, chunk)],
-            out_ref.at[:, pl.ds(part * chunk, chunk)],
-            sems.at[part],
-        )
-
-    def inner(x, carry):
-        second(x + 2, [field_ref[1, c, x] for c in range(3)])
-        return carry
-
-    done = 0
-    for part in range(parts):
-        until = min(width, (part + 1) * chunk + 1)
-        lax.fori_loop(done, until, inner, 0)
-        done = until
-        if part == parts - 1:
-            second(width + 2, [halo_ref[1, 27 + c] for c in range(3)])
-        copy(part).start()
-    for part in range(parts):
-        copy(part).wait()
+        lax.fori_loop(0, 2, edge, 0)
+
+    second(1, [halo_ref[0, 27 + c] for c in range(3)], rate, state, ring, result)
+    second(2, [field_ref[1, c, 0] for c in range(3)], rate, state, ring, result)
+    first = write_out(result, out_ref, sems.at[0], 0, 2)
+    first.start()
+    second(width + 1, [field_ref[1, c, width - 1] for c in range(3)], rate, state, ring, result)
+    second(width + 2, [halo_ref[1, 27 + c] for c in range(3)], rate, state, ring, result)
+    last = write_out(result, out_ref, sems.at[1], width - 2, 2)
+    last.start()
+    first.wait()
+    last.wait()
 
 
 def cost(flops, moved):
@@ -401,20 +515,29 @@
     spans = lax.axis_size("span")
     markers = marker_cells.shape[1]
     held = functools.partial(pltpu.with_memory_space_constraint, memory_space=pltpu.VMEM)
+    far = functools.partial(pltpu.with_memory_space_constraint, memory_space=pltpu.HBM)
     near = lambda *shape: pltpu.VMEM(shape, F32)
     sent = pl.pallas_call(
         bin_kernel,
         out_shape=near(leaves, 3, 128),
-        in_specs=[WHOLE] * 3,
+        in_specs=[HBM] * 3,
         out_specs=WHOLE,
+        scratch_shapes=[
+            pltpu.VMEM((3, 2, markers), F32),
+            pltpu.VMEM((2, 1, markers), jnp.int32),
+            pltpu.VMEM((2, markers), jnp.int32),
+            pltpu.SemaphoreType.DMA((3,)),
+        ],
         compiler_params=params(16),
         name="bin_markers",
     )(
-        jnp.transpose(marker_forces, (1, 0, 2)),
-        jnp.transpose(marker_dest, (0, 2, 1)),
-        marker_cells,
-    )
-    received = lax.all_to_all(sent, "leaf", 0, 0, tiled=True)
+        far(jnp.transpose(marker_forces, (1, 0, 2))),
+        far(jnp.transpose(marker_dest, (0, 2, 1))),
+        far(marker_cells),
+    )
+    received = lax.all_to_all(
+        sent, "leaf", 0, 0, tiled=True, axis_index_groups=[group_order(leaves)]
+    )
     block = 2
     collided = pl.pallas_call(
         first_kernel,
@@ -432,43 +555,76 @@
     )(relax_rates, sent, populations)
     parity = lax.rem(lax.axis_index("span"), 2).astype(jnp.int32).reshape(1)
     layer = near(30, height, length)
-    field, a_sent, b_sent = pl.pallas_call(
+    own = near(30, width, length)
+    field, a_sent, b_sent, up, down = pl.pallas_call(
         deposit_kernel,
-        out_shape=[near(2, 3, width, height, length), layer, layer],
+        out_shape=[near(2, 3, width, height, length), layer, layer, own, own],
         in_specs=[SCALARS, WHOLE, WHOLE],
-        out_specs=[WHOLE] * 3,
+        out_specs=[WHOLE] * 5,
         compiler_params=params(24),
         name="deposit",
     )(parity, held(received), held(collided))
     a_pairs = [(s, s ^ 1) for s in range(spans)]
     b_pairs = [(s, (s + 1 if s % 2 else s - 1) % spans) for s in range(spans)]
+    b_got = lax.ppermute(b_sent, "span", b_pairs)
     a_got = lax.ppermute(a_sent, "span", a_pairs)
-    b_got = lax.ppermute(b_sent, "span", b_pairs)
     face = near(30, 24, length)
-    halo, up, down = pl.pallas_call(
-        pack_kernel,
-        out_shape=[near(2, 30, height, length), face, face],
-        in_specs=[SCALARS] + [WHOLE] * 4,
+    upward = [(l, (l + 1) % leaves) for l in range(leaves)]
+    downward = [(l, (l - 1) % leaves) for l in range(leaves)]
+    low = lax.ppermute(up, "leaf", upward)
+    high = lax.ppermute(down, "leaf", downward)
+    padded = near(27, PLANES, height, length)
+    final = pltpu.HBM(populations.shape, F32)
+    faces = [held(each) for each in (up, down, low, high)]
+    work = 27 * 12 * width * height * length
+    out, state, result, ring = pl.pallas_call(
+        inner_kernel,
+        out_shape=[final, padded, padded, near(2, 9, 24, length)],
+        in_specs=[SCALARS] + [WHOLE] * 6,
+        out_specs=[HBM] + [WHOLE] * 3,
+        scratch_shapes=[pltpu.SemaphoreType.DMA((SPLIT // 2,))],
+        compiler_params=params(16),
+        cost_estimate=cost(work, 4 * populations.size),
+        name="first_planes",
+    )(relax_rates, held(collided), held(field), *faces)
+    corner = near(15, 8, length)
+    halo, up_corner, down_corner = pl.pallas_call(
+        corner_kernel,
+        out_shape=[near(2, 30, height, length), corner, corner],
+        in_specs=[SCALARS] + [WHOLE] * 2 + [HBM],
         out_specs=[WHOLE] * 3,
         compiler_params=params(16),
-        name="pack_layers",
-    )(parity, held(collided), held(field), held(a_got), held(b_got))
-    low = lax.ppermute(up, "leaf", [(l, (l + 1) % leaves) for l in range(leaves)])
-    high = lax.ppermute(down, "leaf", [(l, (l - 1) % leaves) for l in range(leaves)])
+        name="corners",
+    )(parity, held(a_got), held(b_got), ring)
+    low_corner = lax.ppermute(up_corner, "leaf", upward)
+    high_corner = lax.ppermute(down_corner, "leaf", downward)
+    out, result = pl.pallas_call(
+        more_kernel,
+        out_shape=[final, padded],
+        in_specs=[SCALARS] + [WHOLE] * 4 + [HBM],
+        out_specs=[HBM, WHOLE],
+        input_output_aliases={4: 1, 5: 0},
+        scratch_shapes=[pltpu.SemaphoreType.DMA((width // 2,))],
+        compiler_params=params(16),
+        cost_estimate=cost(work, 4 * populations.size),
+        name="more_planes",
+    )(relax_rates, held(state), held(field), held(ring), held(result), far(out))
+    corners = [held(each) for each in (up_corner, down_corner, low_corner, high_corner)]
     return pl.pallas_call(
-        final_kernel,
-        out_shape=jax.ShapeDtypeStruct(populations.shape, F32),
-        in_specs=[SCALARS] + [WHOLE] * 7,
-        out_specs=HBM,
+        outer_kernel,
+        out_shape=[final, padded, padded],
+        in_specs=[SCALARS, WHOLE, WHOLE, WHOLE, HBM] + [WHOLE] * 9,
+        out_specs=[HBM, WHOLE, WHOLE],
+        input_output_aliases={2: 1, 3: 2, 4: 0},
         scratch_shapes=[
-            pltpu.VMEM((27, PLANES, height, length), F32),
+            pltpu.VMEM((2, 30, 24, length), F32),
             pltpu.VMEM((2, 9, 24, length), F32),
-            pltpu.VMEM((27, PLANES, height, length), F32),
-            pltpu.SemaphoreType.DMA((width // 4,)),
+            pltpu.VMEM((2, 9, 24, length), F32),
+            pltpu.SemaphoreType.DMA((2,)),
         ],
-        compiler_params=params(32),
-        name="collide_second",
-    )(relax_rates, held(collided), held(field), held(halo), held(up), held(down), held(low), held(high))
+        compiler_params=params(16),
+        name="outer_planes",
+    )(relax_rates, held(halo), held(state), held(result), far(out), held(field), *faces, *corners)[0]
 
 
 def solution(mesh):

time: 64.4 us -> 51.7 us (0.80)
  waiting for transfers between devices: 19.2 us -> 2.52 us
  Pallas kernels: 11.3 us -> 14.6 us
  starting transfers between devices: 29.2 us -> 31.6 us
  local copies, waits for them, and re-layouts: 4.2 us -> 2.13 us
    all_to_all x1, waiting for transfers between devices: 9.25 us -> 2.19 us  [body(): lax.all_to_all(sent, 'leaf', 0, 0, tiled=True, axis_index_groups=[group_o...]
    ppermute x2 -> x4, waiting for transfers between devices: 7.23 us -> 0.32 us  [the longest x1 0.31 us: body(): high_corner = lax.ppermute(down_corner, 'leaf', downward)]
    ppermute x1, waiting for transfers between devices: 2.75 us -> 0.01 us  [body(): b_got = lax.ppermute(b_sent, 'span', b_pairs)]
    pallas_call x3 -> x5, Pallas kernels: 8.08 us -> 10.7 us  [the longest x1 4.09 us: body(): pl.pallas_call(inner_kernel, out_shape=[final, padded, padded, near(2, 9,...]
    unnamed x12 -> x6, local copies, waits for them, and re-layouts: 4.2 us -> 2.13 us
    all_to_all x1, starting transfers between devices: 16.7 us -> 18.3 us  [body(): lax.all_to_all(sent, 'leaf', 0, 0, tiled=True, axis_index_groups=[group_o...]
    ppermute x2 -> x4, starting transfers between devices: 3.19 us -> 3.96 us  [the longest x1 2.32 us: body(): low_corner = lax.ppermute(up_corner, 'leaf', upward)]
    pallas_call x1, Pallas kernels: 1.54 us -> 2.22 us  [body(): pl.pallas_call(deposit_kernel, out_shape=[near(2, 3, width, height, lengt...]
  transfers between devices with their start and end apart: 5 -> 7, of which waited for: 4 -> 2; matrix products, arithmetic and copies ran while one was open for 0% -> 0% of each run, Pallas kernels for 3% -> 16%
where the time goes in v2:
time: 51.7 us; the launch traced here: 51 us
  starting transfers between devices  31.6 us (61%)
  Pallas kernels  14.6 us (28%)
  waiting for transfers between devices  2.52 us (5%)
  local copies, waits for them, and re-layouts  2.13 us (4%)
    all_to_all x1, starting transfers between devices, body(): lax.all_to_all(sent, 'leaf', 0, 0, tiled=True, axis_index_groups=[group_o...  18.3 us
    ppermute x1, starting transfers between devices, body(): b_got = lax.ppermute(b_sent, 'span', b_pairs)  6.17 us
    pallas_call x1, Pallas kernels, body(): pl.pallas_call(inner_kernel, out_shape=[final, padded, padded, near(2, 9,...  4.09 us
    ppermute x1, starting transfers between devices, body(): a_got = lax.ppermute(a_sent, 'span', a_pairs)  3.12 us
    pallas_call x1, Pallas kernels, body(): pl.pallas_call(more_kernel, out_shape=[final, padded], in_specs=[SCALARS]...  2.39 us
    ppermute x1, starting transfers between devices, body(): low_corner = lax.ppermute(up_corner, 'leaf', upward)  2.32 us
    pallas_call x1, Pallas kernels, body(): pl.pallas_call(deposit_kernel, out_shape=[near(2, 3, width, height, lengt...  2.22 us
    all_to_all x1, waiting for transfers between devices, body(): lax.all_to_all(sent, 'leaf', 0, 0, tiled=True, axis_index_groups=[group_o...  2.19 us
  transfers between devices with their start and end apart: 7, of which 2 were waited for; matrix products, arithmetic and copies ran while one was open for 0% of the time, Pallas kernels for 16%

profile of v2, /device:TPU:1, one launch (start us, length us, event | category | flops | bytes accessed | tf_op | source)
XLA Modules:
  0.0 51.0 jit_solution(2090490148074547831)
XLA Ops:
  0.0 2.1 %bin_markers.1.after_ref = f32[32,3,128]{2,1,0:T(4,128)} custom-call(f32[3,2,384]{2,1,0:T(2,128)} %bitcast.3, s32[2,1,384]{2,1,0:T(1,128)} %bitcast.4, s32[2,384]{1,0:T(2,128)} %cells_hbm.1), custom_call_target="tpu_custom_call" | custom-call | tf_op jit(solution)/shard_map/bin_markers/pallas_call | solution.py:520
  2.1 18.3 %all-to-all-start = ((f32[32,3,128]{2,1,0:T(4,128)}), f32[32,3,128]{2,1,0:T(4,128)S(1)}, u32[]{:S(2)}, u32[]{:S(2)}) async-start(f32[32,3,128]{2,1,0:T(4,128)} %bin_markers.1.after_ref), calls=%async_computation | async-start | bytes 131072 | tf_op jit(solution)/shard_map/all_to_all | solution.py:538
  20.4 0.0 copy-start
  20.4 1.5 %copy-done = f32[27,16,8,128]{3,2,1,0:T(8,128)S(1)} copy-done((f32[27,16,8,128]{3,2,1,0:T(8,128)S(1)}, f32[27,16,8,128]{3,2,1,0:T(8,128)}, u32[]{:S(2)}) %copy-start) | copy-done | bytes 1769496
  21.9 0.7 %copy-done.1 = f32[27]{0:T(128)S(1)} copy-done((f32[27]{0:T(128)S(1)}, f32[27]{0:T(128)}, u32[]{:S(2)}) %copy-start.1) | copy-done | bytes 132
  22.6 1.7 %collide_first.1.collided_ref = f32[27,16,8,128]{3,2,1,0:T(8,128)S(1)} custom-call(f32[27]{0:T(128)S(1)} %copy-done.1, f32[32,3,128]{2,1,0:T(4,128)} %bin_markers.1.after_ref, f32[27,16,8,128]{3,2,1,0:T(8,128)S(1)} %copy-done), custom_call_target="tpu_custom_call" | custom-call | flops 5308416 | bytes 3538944 | tf_op jit(solution)/shard_map/collide_first/pallas_call | solution.py:542
  24.2 2.2 %all-to-all-done.received_ref = f32[32,3,128]{2,1,0:T(4,128)S(1)} async-done(((f32[32,3,128]{2,1,0:T(4,128)}), f32[32,3,128]{2,1,0:T(4,128)S(1)}, u32[]{:S(2)}, u32[]{:S(2)}) %all-to-all-start) | async-done | bytes 49184 | tf_op jit(solution)/shard_map/all_to_all | solution.py:538
  26.4 2.2 %deposit.1 = (f32[2,3,16,8,128]{4,3,2,1,0:T(8,128)S(1)}, f32[30,8,128]{2,1,0:T(8,128)S(1)}, f32[30,8,128]{2,1,0:T(8,128)S(1)}, f32[30,16,128]{2,1,0:T(8,128)S(1)}, f32[30,16,128]{2,1,0:T(8,128)S(1)}) custom-call(s32[1]{0:T(128)} %bitcast.parity_ref, f32[32,3,128]{2,1,0:T(4,128)S(1)} %all-to-all-done.received_ref, ...), custom_call_target="tpu_custom_call" | custom-call | tf_op jit(solution)/shard_map/deposit/pallas_call | solution.py:559
  28.7 0.7 %collective-permute-start.2 = (f32[30,16,128]{2,1,0:T(8,128)S(1)}, f32[30,16,128]{2,1,0:T(8,128)S(1)}, u32[]{:S(2)}, u32[]{:S(2)}) collective-permute-start(f32[30,16,128]{2,1,0:T(8,128)S(1)} %get-tuple-element.23.up_ref), channel_id=1, source_target_pairs={{0,1},{1,2},{2,3},{3,4},{4,5},{5,6},{6,7},{7,8},{8,9},{9,10},{10,1... | collective-permute-start | bytes 737288 | tf_op jit(solution)/shard_map/ppermute | solution.py:574
  29.4 0.0 collective-permute-start.3
  29.4 3.1 %collective-permute-start = (f32[30,8,128]{2,1,0:T(8,128)S(1)}, f32[30,8,128]{2,1,0:T(8,128)S(1)}, u32[]{:S(2)}, u32[]{:S(2)}) collective-permute-start(f32[30,8,128]{2,1,0:T(8,128)S(1)} %get-tuple-element.20), channel_id=1, source_target_pairs={{0,32},{32,0},{64,96},{96,64},{128,160},{160,128},{192,224},{224,1... | collective-permute-start | bytes 368648 | tf_op jit(solution)/shard_map/ppermute | solution.py:570
  32.5 6.2 %collective-permute-start.1 = (f32[30,8,128]{2,1,0:T(8,128)S(1)}, f32[30,8,128]{2,1,0:T(8,128)S(1)}, u32[]{:S(2)}, u32[]{:S(2)}) collective-permute-start(f32[30,8,128]{2,1,0:T(8,128)S(1)} %get-tuple-element.21), channel_id=1, source_target_pairs={{0,480},{32,64},{64,32},{96,128},{128,96},{160,192},{192,160},{224... | collective-permute-start | bytes 368648 | tf_op jit(solution)/shard_map/ppermute | solution.py:569
  38.7 0.0 collective-permute-done.2.low_ref
  38.7 0.0 collective-permute-done.3.high_ref
  38.7 4.1 %first_planes.1 = (f32[27,16,8,128]{3,2,1,0:T(8,128)}, f32[27,20,8,128]{3,2,1,0:T(8,128)S(1)}, f32[27,20,8,128]{3,2,1,0:T(8,128)S(1)}, f32[2,9,24,128]{3,2,1,0:T(8,128)S(1)}) custom-call(f32[27]{0:T(128)S(1)} %copy-done.2, f32[27,16,8,128]{3,2,1,0:T(8,128)S(1)} %collide_first.1.collided_ref, f32[2,3,16,8,128]{4,3,2,1,0:T(8,128)S(1)} %get-tuple-element.22.field_ref, ...), custom_call_target="tpu_custom_call" | custom-call | flops 5308416 | bytes 1769472 | tf_op jit(solution)/shard_map/first_planes/pallas_call | solution.py:580
  42.8 0.0 collective-permute-done.a_ref
  42.8 0.0 collective-permute-done.1.b_ref
  42.8 0.1 corners.1
  42.9 2.3 %collective-permute-start.4 = (f32[15,8,128]{2,1,0:T(8,128)S(1)}, f32[15,8,128]{2,1,0:T(8,128)S(1)}, u32[]{:S(2)}, u32[]{:S(2)}) collective-permute-start(f32[15,8,128]{2,1,0:T(8,128)S(1)} %get-tuple-element.32.up_corner), channel_id=1, source_target_pairs={{0,1},{1,2},{2,3},{3,4},{4,5},{5,6},{6,7},{7,8},{8,9},{9,10},{10,1... | collective-permute-start | bytes 184328 | tf_op jit(solution)/shard_map/ppermute | solution.py:599
  45.2 0.9 %collective-permute-start.5 = (f32[15,8,128]{2,1,0:T(8,128)S(1)}, f32[15,8,128]{2,1,0:T(8,128)S(1)}, u32[]{:S(2)}, u32[]{:S(2)}) collective-permute-start(f32[15,8,128]{2,1,0:T(8,128)S(1)} %get-tuple-element.33.down_corner), channel_id=1, source_target_pairs={{0,31},{1,0},{2,1},{3,2},{4,3},{5,4},{6,5},{7,6},{8,7},{9,8},{10,9... | collective-permute-start | bytes 184328 | tf_op jit(solution)/shard_map/ppermute | solution.py:600
  46.2 2.4 %more_planes.1 = (f32[27,16,8,128]{3,2,1,0:T(8,128)}, f32[27,20,8,128]{3,2,1,0:T(8,128)S(1)}) custom-call(f32[27]{0:T(128)S(1)} %copy-done.2, f32[27,20,8,128]{3,2,1,0:T(8,128)S(1)} %get-tuple-element.27.state.state_in, f32[2,3,16,8,128]{4,3,2,1,0:T(8,128)S(1)} %get-tuple-element.22.field_ref, ...), custom_call_target="tpu_custom_call", output_to_operand_aliasing={{1}: (4, {}), {0}: (5, {})} | custom-call | flops 5308416 | bytes 1769472 | tf_op jit(solution)/shard_map/more_planes/pallas_call | solution.py:601
  48.6 0.0 collective-permute-done.4.low_corner
  48.6 0.3 collective-permute-done.5.high_corner
  48.9 2.1 %outer_planes.1 = (f32[27,16,8,128]{3,2,1,0:T(8,128)}, f32[27,20,8,128]{3,2,1,0:T(8,128)S(1)}, f32[27,20,8,128]{3,2,1,0:T(8,128)S(1)}) custom-call(f32[27]{0:T(128)S(1)} %copy-done.2, f32[2,30,8,128]{3,2,1,0:T(8,128)S(1)} %get-tuple-element.26.halo_ref, ...), custom_call_target="tpu_custom_call", output_to_operand_aliasing={{1}: (2, {}), {2}: (3, {}), {0}: (4, {})} | custom-call | tf_op jit(solution)/shard_map/outer_planes/pallas_call | solution.py:613
  (3 shorter events, 0.0 us)
Async XLA Ops:
  2.1 24.4 %all-to-all-start = ((f32[32,3,128]{2,1,0:T(4,128)}), f32[32,3,128]{2,1,0:T(4,128)S(1)}, u32[]{:S(2)}, u32[]{:S(2)}) async-start(f32[32,3,128]{2,1,0:T(4,128)} %bin_markers.1.after_ref), calls=%async_computation | async-start | bytes 131072 | tf_op jit(solution)/shard_map/all_to_all | solution.py:538
  20.4 1.5 %copy-start = (f32[27,16,8,128]{3,2,1,0:T(8,128)S(1)}, f32[27,16,8,128]{3,2,1,0:T(8,128)}, u32[]{:S(2)}) copy-start(f32[27,16,8,128]{3,2,1,0:T(8,128)} %populations_ref.1) | copy-start | bytes 5308420
  21.9 0.7 %copy-start.1 = (f32[27]{0:T(128)S(1)}, f32[27]{0:T(128)}, u32[]{:S(2)}) copy-start(f32[27]{0:T(128)} %rates_ref.7) | copy-start | bytes 328
  22.6 16.1 %copy-start.2 = (f32[27]{0:T(128)S(1)}, f32[27]{0:T(128)}, u32[]{:S(2)}) copy-start(f32[27]{0:T(128)} %rates_ref.7) | copy-start | bytes 328
  28.7 10.0 %collective-permute-start.2 = (f32[30,16,128]{2,1,0:T(8,128)S(1)}, f32[30,16,128]{2,1,0:T(8,128)S(1)}, u32[]{:S(2)}, u32[]{:S(2)}) collective-permute-start(f32[30,16,128]{2,1,0:T(8,128)S(1)} %get-tuple-element.23.up_ref), channel_id=1, source_target_pairs={{0,1},{1,2},{2,3},{3,4},{4,5},{5,6},{6,7},{7,8},{8,9},{9,10},{10,1... | collective-permute-start | bytes 737288 | tf_op jit(solution)/shard_map/ppermute | solution.py:574
  29.4 9.3 %collective-permute-start.3 = (f32[30,16,128]{2,1,0:T(8,128)S(1)}, f32[30,16,128]{2,1,0:T(8,128)S(1)}, u32[]{:S(2)}, u32[]{:S(2)}) collective-permute-start(f32[30,16,128]{2,1,0:T(8,128)S(1)} %get-tuple-element.24.down_ref), channel_id=1, source_target_pairs={{0,31},{1,0},{2,1},{3,2},{4,3},{5,4},{6,5},{7,6},{8,7},{9,8},{10,9... | collective-permute-start | bytes 737288 | tf_op jit(solution)/shard_map/ppermute | solution.py:575
  29.4 13.4 %collective-permute-start = (f32[30,8,128]{2,1,0:T(8,128)S(1)}, f32[30,8,128]{2,1,0:T(8,128)S(1)}, u32[]{:S(2)}, u32[]{:S(2)}) collective-permute-start(f32[30,8,128]{2,1,0:T(8,128)S(1)} %get-tuple-element.20), channel_id=1, source_target_pairs={{0,32},{32,0},{64,96},{96,64},{128,160},{160,128},{192,224},{224,1... | collective-permute-start | bytes 368648 | tf_op jit(solution)/shard_map/ppermute | solution.py:570
  32.5 10.3 %collective-permute-start.1 = (f32[30,8,128]{2,1,0:T(8,128)S(1)}, f32[30,8,128]{2,1,0:T(8,128)S(1)}, u32[]{:S(2)}, u32[]{:S(2)}) collective-permute-start(f32[30,8,128]{2,1,0:T(8,128)S(1)} %get-tuple-element.21), channel_id=1, source_target_pairs={{0,480},{32,64},{64,32},{96,128},{128,96},{160,192},{192,160},{224... | collective-permute-start | bytes 368648 | tf_op jit(solution)/shard_map/ppermute | solution.py:569
  42.9 5.6 %collective-permute-start.4 = (f32[15,8,128]{2,1,0:T(8,128)S(1)}, f32[15,8,128]{2,1,0:T(8,128)S(1)}, u32[]{:S(2)}, u32[]{:S(2)}) collective-permute-start(f32[15,8,128]{2,1,0:T(8,128)S(1)} %get-tuple-element.32.up_corner), channel_id=1, source_target_pairs={{0,1},{1,2},{2,3},{3,4},{4,5},{5,6},{6,7},{7,8},{8,9},{9,10},{10,1... | collective-permute-start | bytes 184328 | tf_op jit(solution)/shard_map/ppermute | solution.py:599
  45.2 3.6 %collective-permute-start.5 = (f32[15,8,128]{2,1,0:T(8,128)S(1)}, f32[15,8,128]{2,1,0:T(8,128)S(1)}, u32[]{:S(2)}, u32[]{:S(2)}) collective-permute-start(f32[15,8,128]{2,1,0:T(8,128)S(1)} %get-tuple-element.33.down_corner), channel_id=1, source_target_pairs={{0,31},{1,0},{2,1},{3,2},{4,3},{5,4},{6,5},{7,6},{8,7},{9,8},{10,9... | collective-permute-start | bytes 184328 | tf_op jit(solution)/shard_map/ppermute | solution.py:600

commit v3 on v2

--- a/solution.py
+++ b/solution.py
@@ -128,7 +128,6 @@
     markers = cells_ref.shape[1]
     leaves = sent_ref.shape[0]
     root = leaves * 5 // 8
-    highest = lax.Precision.HIGHEST
     earlier = (
         lax.broadcasted_iota(jnp.int32, (markers, markers), 0)
         < lax.broadcasted_iota(jnp.int32, (markers, markers), 1)
@@ -156,15 +155,21 @@
         own = jnp.concatenate([jnp.where(spot, row, 0.0) for row in rows], axis=0)
         none = jnp.zeros_like(own)
         right.append(jnp.concatenate([own, none] if t == 0 else [none, own], axis=0))
+    values = jnp.concatenate(right, axis=1)
+    parts = []
+    for _ in range(3):
+        part = values.astype(BF16)
+        parts.append(part)
+        values = values - part.astype(F32)
     packed = lax.dot_general(
-        jnp.concatenate(left, axis=1),
-        jnp.concatenate(right, axis=1),
+        jnp.concatenate(left, axis=1).astype(BF16),
+        jnp.concatenate(parts, axis=0),
         (((1,), (1,)), ((), ())),
-        precision=highest,
         preferred_element_type=F32,
     )
+    packed = packed[:, :128] + packed[:, 128:256] + packed[:, 256:]
     for r in range(3):
-        sent_ref[:, r, :] = packed[r * leaves : (r + 1) * leaves]
+        sent_ref[:, 0, 128 * r : 128 * r + 128] = packed[r * leaves : (r + 1) * leaves]
 
 
 def first_kernel(rates_ref, after_ref, populations_ref, collided_ref):
@@ -185,7 +190,7 @@
 def rows_by_value(received_ref):
     blocks = []
     for r in range(2):
-        whole = received_ref[:, r, :]
+        whole = received_ref[:, 0, 128 * r : 128 * r + 128]
         blocks += [whole[8 * b : 8 * b + 8] for b in range(4)]
     lane = lax.broadcasted_iota(jnp.int32, (8, 128), 1)
     for half in (4, 2, 1):
@@ -196,7 +201,7 @@
             first, second = blocks[b], blocks[b + half]
             blocks[b] = jnp.where(low, first, pltpu.roll(second, 16 * half, 1))
             blocks[b + half] = jnp.where(low, pltpu.roll(first, 128 - 16 * half, 1), second)
-    last = received_ref[:, 2, :]
+    last = received_ref[:, 0, 256:384]
     tail = None
     for b in range(4):
         part = last[8 * b : 8 * b + 8]
@@ -232,9 +237,7 @@
             ref[27 + c] = field_ref[1, c, :, height - 1 if sign > 0 else 0, :]
 
 
-def deposit_kernel(
-    parity_ref, received_ref, collided_ref, field_ref, a_ref, b_ref, up_ref, down_ref
-):
+def deposit_kernel(received_ref, collided_ref, field_ref, up_ref, down_ref):
     rows = rows_by_value(received_ref)
     index = lax.broadcasted_iota(jnp.int32, (128, 128), 0).astype(F32).astype(BF16)
     one, zero = jnp.ones((), BF16), jnp.zeros((), BF16)
@@ -256,27 +259,47 @@
                 jnp.concatenate([p[0] for p in parts] + [p[1] for p in parts], axis=0)
             )
         field = lax.dot_general(
+            jnp.concatenate(weighted, axis=1),
             jnp.concatenate(outer, axis=1),
-            jnp.concatenate(weighted, axis=1),
             (((1,), (1,)), ((), ())),
             preferred_element_type=F32,
         )
         for c in range(3):
-            whole = field[:, 128 * c : 128 * c + 128] + field[:, 384 + 128 * c : 512 + 128 * c]
-            field_ref[t, c] = whole.reshape(field_ref.shape[2:])
+            whole = field[128 * c : 128 * c + 128] + field[384 + 128 * c : 512 + 128 * c]
+            field_ref[t, c] = whole.T.reshape(field_ref.shape[2:])
+    own_faces(collided_ref, field_ref, up_ref, down_ref)
+
+
+def corner_at(place, number):
+    return place // 2, pl.ds(4 * (place % 2) + number, 1)
+
+
+def side_kernel(parity_ref, collided_ref, field_ref, after_ref, low_ref, high_ref, a_ref, b_ref):
     last = collided_ref.shape[1] - 1
 
     def layers(ref, sign, edge, inside):
-        terms = sources([field_ref[0, c, edge] for c in range(3)])
-        for n in range(18):
-            q = 9 + n if n < 9 else 9 + 9 * sign + n - 9
-            ref[n] = pushed(collided_ref[q, edge], terms[q])
-        terms = sources([field_ref[0, c, inside] for c in range(3)])
-        for n in range(9):
-            q = 9 + 9 * sign + n
-            ref[18 + n] = pushed(collided_ref[q, inside], terms[q])
+        def put(n, number, got, place, x):
+            tile, row = corner_at(n, number)
+            ref[30 + tile, row, :] = got[place, pl.ds(x, 1), :]
+
+        for first, count, x in ((0, 18, edge), (18, 9, inside)):
+            terms = sources([field_ref[0, c, x] for c in range(3)])
+            for n in range(first, first + count):
+                q = 9 + n if n < 9 else 9 + 9 * sign + n % 9
+                j, cz = q // 3, q % 3 - 1
+                ref[n] = pushed(collided_ref[q, x], terms[q])
+                if cz >= 0:
+                    put(n, 1, low_ref, 9 * cz + j, x)
+                if cz <= 0:
+                    put(n, 2, high_ref, -9 * cz + j, x)
+                if cz > 0:
+                    put(n, 0, low_ref, 18 + j, x)
+                if cz < 0:
+                    put(n, 3, high_ref, 18 + j, x)
         for c in range(3):
             ref[27 + c] = field_ref[1, c, edge]
+            put(27 + c, 1, low_ref, 27 + c, edge)
+            put(27 + c, 2, high_ref, 27 + c, edge)
 
     @pl.when(parity_ref[0] == 0)
     def _():
@@ -288,14 +311,11 @@
         layers(b_ref, 1, last, last - 1)
         layers(a_ref, -1, 0, 1)
 
-    own_faces(collided_ref, field_ref, up_ref, down_ref)
-
-
-def corner_at(place, number):
-    return place // 2, pl.ds(4 * (place % 2) + number, 1)
-
-
-def corner_kernel(parity_ref, a_ref, b_ref, after_ref, halo_ref, up_ref, down_ref):
+
+def corner_kernel(
+    parity_ref, a_ref, b_ref, after_ref,
+    halo_ref, up_ref, down_ref, low_ref, high_ref,
+):
     @pl.when(parity_ref[0] == 0)
     def _():
         halo_ref[0] = b_ref[...]
@@ -307,28 +327,38 @@
         halo_ref[1] = b_ref[...]
 
     height = a_ref.shape[1]
-    for ref, sign in ((up_ref, 1), (down_ref, -1)):
-
-        def put(place, number, side, layer, z):
-            tile, row = corner_at(place, number)
-            ref[tile, row, :] = halo_ref[side, layer, pl.ds(z, 1), :]
-
-        for z, first, kinds in rows_of(height, sign):
-            for order, cz in enumerate(kinds):
-                for j in range(9):
-                    place = first + 9 * order + j
-                    cx = j // 3 - 1
-                    n = 3 * (j % 3) + cz + 1
-                    for side, toward, near, far in ((0, 1, 1, 0), (1, -1, 2, 3)):
-                        if cx == 0:
-                            put(place, near, side, n, z)
-                        if cx == toward:
-                            put(place, near, side, 9 + n, z)
-                            put(place, far, side, 18 + n, z)
-        edge = height - 1 if sign > 0 else 0
+
+    def columns(place, cz, load, ref):
+        cx = (place % 9) // 3 - 1
+        n = 3 * (place % 3) + cz + 1
+        for side, toward, near, far in ((0, 1, 1, 0), (1, -1, 2, 3)):
+            wanted = [(near, n)] if cx == 0 else []
+            if cx == toward:
+                wanted = [(near, 9 + n), (far, 18 + n)]
+            for number, layer in wanted:
+                tile, row = corner_at(place, number)
+                ref[tile, row, :] = load(side, layer)
+
+    def outside(number):
+        def load(side, layer):
+            tile, row = corner_at(layer, number)
+            return halo_ref[side, 30 + tile, row, :]
+
+        return load
+
+    for ref, own_ref, sign, first, z in (
+        (low_ref, down_ref, 1, 1, 0),
+        (high_ref, up_ref, -1, 2, height - 1),
+    ):
+        for j in range(9):
+            columns(j, 0, outside(first), ref)
+            columns(9 + j, sign, outside(first), ref)
+            columns(18 + j, sign, outside(first - sign), ref)
+            columns(9 + j, -sign, lambda side, n: halo_ref[side, n, pl.ds(z, 1), :], own_ref)
         for c in range(3):
-            put(27 + c, 1, 0, 27 + c, edge)
-            put(27 + c, 2, 1, 27 + c, edge)
+            for side, number in ((0, 1), (1, 2)):
+                tile, row = corner_at(27 + c, number)
+                ref[tile, row, :] = outside(first)(side, 27 + c)
 
 
 def moved(tile, q, low_row, high_row):
@@ -360,15 +390,16 @@
     return [after[3 * j + toward + 1] for j in range(9)]
 
 
-def second(x, force, rate, state, ring, result):
+def second(x, force, rate, state, ring, result, row=None):
+    row = x if row is None else row
     after = collide([state[q, x] for q in range(27)], rate, force)
     for q in range(27):
         j = q // 3
         result[q, x + q // 9 - 1] = moved(
             after[q],
             q,
-            lambda: ring[0, j, pl.ds(x, 1), :],
-            lambda: ring[1, j, pl.ds(x, 1), :],
+            lambda: ring[0, j, pl.ds(row, 1), :],
+            lambda: ring[1, j, pl.ds(row, 1), :],
         )
 
 
@@ -378,43 +409,43 @@
     )
 
 
-def planes(first, last, rate, field_ref, state, ring, result, out_ref, sems):
+def planes(first, last, rate, field_ref, state, ring, result):
     def plane(x, carry):
         second(x + 2, [field_ref[1, c, x] for c in range(3)], rate, state, ring, result)
         return carry
 
-    copies = []
-    done = first
-    for place in range(max(2, first - 1), last - 2, 2):
-        lax.fori_loop(done, place + 3, plane, 0)
-        done = place + 3
-        copies.append(write_out(result, out_ref, sems.at[len(copies)], place, 2))
-        copies[-1].start()
-    for each in copies:
-        each.wait()
-
-
-def inner_kernel(
-    rates_ref, collided_ref, field_ref, up_ref, down_ref, low_ref, high_ref,
-    out_ref, state, result, ring, sems,
-):
-    width = collided_ref.shape[1]
-    rate = lambda k: rates_ref[k]
-
+    lax.fori_loop(first, last, plane, 0)
+
+
+def stream_kernel(collided_ref, field_ref, state):
     def own(x, carry):
         terms = sources([field_ref[0, c, x] for c in range(3)])
         for q in range(27):
-            place = 9 + q // 3
+            cx, cy, cz = components(q)
             tile = pushed(collided_ref[q, x], terms[q])
-            state[q, x + 2 + q // 9 - 1] = moved(
-                tile,
-                q,
-                lambda: low_ref[place, pl.ds(x, 1), :],
-                lambda: high_ref[place, pl.ds(x, 1), :],
-            )
+            if cz:
+                tile = pltpu.roll(tile, cz % tile.shape[0], 0)
+            if cy:
+                tile = pltpu.roll(tile, cy % 128, 1)
+            state[q, x + 2 + cx] = tile
         return carry
 
-    lax.fori_loop(0, width, own, 0)
+    lax.fori_loop(0, collided_ref.shape[1], own, 0)
+
+
+def inner_kernel(
+    rates_ref, state_in, field_ref, up_ref, down_ref, low_ref, high_ref,
+    state, result, ring,
+):
+    width, height = field_ref.shape[2:4]
+    rate = lambda k: rates_ref[k]
+    for q in range(27):
+        cx, cy, cz = components(q)
+        if cz == 0:
+            continue
+        got, z = (low_ref, 0) if cz > 0 else (high_ref, height - 1)
+        rows = got[9 + q // 3]
+        state[q, pl.ds(2 + cx, width), z, :] = pltpu.roll(rows, cy % 128, 1) if cy else rows
     for side, got, sent, toward in ((0, low_ref, down_ref, 1), (1, high_ref, up_ref, -1)):
 
         def edge(block, carry, side=side, got=got, sent=sent, toward=toward):
@@ -430,15 +461,23 @@
             return carry
 
         lax.fori_loop(0, 2, edge, 0)
-    planes(1, SPLIT, rate, field_ref, state, ring, result, out_ref, sems)
-
-
-def more_kernel(
-    rates_ref, state, field_ref, ring, result_in, out_in, out_ref, result, sems
-):
+    planes(1, SPLIT, rate, field_ref, state, ring, result)
+
+
+def more_kernel(rates_ref, state, field_ref, ring, result_in, out_ref, result, sems):
     width = field_ref.shape[2]
     rate = lambda k: rates_ref[k]
-    planes(SPLIT, width - 1, rate, field_ref, state, ring, result, out_ref, sems)
+    copies = [write_out(result, out_ref, sems.at[0], 2, SPLIT - 3)]
+    copies[0].start()
+    done = SPLIT
+    for place in range(SPLIT - 1, width - 4, 2):
+        planes(done, place + 3, rate, field_ref, state, ring, result)
+        done = place + 3
+        copies.append(write_out(result, out_ref, sems.at[len(copies)], place, 2))
+        copies[-1].start()
+    planes(done, width - 1, rate, field_ref, state, ring, result)
+    for each in copies:
+        each.wait()
 
 
 def outer_kernel(
@@ -449,6 +488,8 @@
 ):
     width = field_ref.shape[2]
     rate = lambda k: rates_ref[k]
+    ready = write_out(result, out_ref, sems.at[2], width - 4, 2)
+    ready.start()
     columns = (0, 1, width + 2, width + 3)
     for side, toward, near in ((0, 1, 1), (1, -1, width + 2)):
         for n in range(27):
@@ -464,10 +505,11 @@
             )
 
     def gather(target, place, own, corner, source):
-        target[place, pl.ds(2, width), :] = own[source]
-        for number, column in enumerate(columns):
-            tile, row = corner_at(source, number)
-            target[place, pl.ds(column, 1), :] = corner[tile, row, :]
+        tile, row = source // 2, 4 * (source % 2)
+        target[place, pl.ds(0, 2), :] = corner[tile, pl.ds(row, 2), :]
+        target[place, pl.ds(2, 2), :] = own[source, pl.ds(0, 2), :]
+        target[place, pl.ds(4, 2), :] = own[source, pl.ds(width - 2, 2), :]
+        target[place, pl.ds(6, 2), :] = corner[tile, pl.ds(row + 2, 2), :]
 
     sides = (
         (0, low_ref, low_corner, down_ref, down_corner, 1),
@@ -478,29 +520,35 @@
             gather(got.at[side], place, mine, corner, place)
         for j in range(9):
             gather(sent.at[side], j, left, left_corner, 9 + j)
-
-        def edge(block, carry, side=side, toward=toward):
-            start = 1 + (width - 6) * block
-            force = [got[side, 27 + c, pl.ds(start, 8), :] for c in range(3)]
-            rows = edge_rows(
-                lambda place, where: got[side, place, where, :],
-                lambda place, where: sent[side, place - 9, where, :],
-                toward, start, force, rate,
-            )
-            for j in range(9):
-                ring[side, j, pl.ds(start, 8), :] = rows[j]
-            return carry
-
-        lax.fori_loop(0, 2, edge, 0)
-
-    second(1, [halo_ref[0, 27 + c] for c in range(3)], rate, state, ring, result)
-    second(2, [field_ref[1, c, 0] for c in range(3)], rate, state, ring, result)
+        values = []
+        for q in range(27):
+            cx, cy, cz = components(q)
+            j = q // 3
+            if cz == toward:
+                row = got[side, 18 + j]
+            elif cz == 0:
+                row = got[side, j]
+            else:
+                row = sent[side, j]
+            if cx:
+                row = pltpu.roll(row, cx % 8, 0)
+            values.append(pltpu.roll(row, cy % 128, 1) if cy else row)
+        after = collide(values, rate, [got[side, 27 + c] for c in range(3)])
+        for j in range(9):
+            ring[side, j] = after[3 * j + toward + 1]
+
+    def plane(x, row, force):
+        second(x, force, rate, state, ring, result, row)
+
+    plane(1, 1, [halo_ref[0, 27 + c] for c in range(3)])
+    plane(2, 2, [field_ref[1, c, 0] for c in range(3)])
     first = write_out(result, out_ref, sems.at[0], 0, 2)
     first.start()
-    second(width + 1, [field_ref[1, c, width - 1] for c in range(3)], rate, state, ring, result)
-    second(width + 2, [halo_ref[1, 27 + c] for c in range(3)], rate, state, ring, result)
+    plane(width + 1, 5, [field_ref[1, c, width - 1] for c in range(3)])
+    plane(width + 2, 6, [halo_ref[1, 27 + c] for c in range(3)])
     last = write_out(result, out_ref, sems.at[1], width - 2, 2)
     last.start()
+    ready.wait()
     first.wait()
     last.wait()
 
@@ -519,7 +567,7 @@
     near = lambda *shape: pltpu.VMEM(shape, F32)
     sent = pl.pallas_call(
         bin_kernel,
-        out_shape=near(leaves, 3, 128),
+        out_shape=near(leaves, 1, 384),
         in_specs=[HBM] * 3,
         out_specs=WHOLE,
         scratch_shapes=[
@@ -554,61 +602,73 @@
         name="collide_first",
     )(relax_rates, sent, populations)
     parity = lax.rem(lax.axis_index("span"), 2).astype(jnp.int32).reshape(1)
-    layer = near(30, height, length)
     own = near(30, width, length)
-    field, a_sent, b_sent, up, down = pl.pallas_call(
+    field, up, down = pl.pallas_call(
         deposit_kernel,
-        out_shape=[near(2, 3, width, height, length), layer, layer, own, own],
-        in_specs=[SCALARS, WHOLE, WHOLE],
-        out_specs=[WHOLE] * 5,
+        out_shape=[near(2, 3, width, height, length), own, own],
+        in_specs=[WHOLE, WHOLE],
+        out_specs=[WHOLE] * 3,
         compiler_params=params(24),
         name="deposit",
-    )(parity, held(received), held(collided))
-    a_pairs = [(s, s ^ 1) for s in range(spans)]
-    b_pairs = [(s, (s + 1 if s % 2 else s - 1) % spans) for s in range(spans)]
-    b_got = lax.ppermute(b_sent, "span", b_pairs)
-    a_got = lax.ppermute(a_sent, "span", a_pairs)
-    face = near(30, 24, length)
-    upward = [(l, (l + 1) % leaves) for l in range(leaves)]
-    downward = [(l, (l - 1) % leaves) for l in range(leaves)]
-    low = lax.ppermute(up, "leaf", upward)
-    high = lax.ppermute(down, "leaf", downward)
+    )(held(received), held(collided))
+    low = lax.ppermute(up, "leaf", [(l, (l + 1) % leaves) for l in range(leaves)])
+    high = lax.ppermute(down, "leaf", [(l, (l - 1) % leaves) for l in range(leaves)])
     padded = near(27, PLANES, height, length)
     final = pltpu.HBM(populations.shape, F32)
     faces = [held(each) for each in (up, down, low, high)]
     work = 27 * 12 * width * height * length
-    out, state, result, ring = pl.pallas_call(
+    streamed = pl.pallas_call(
+        stream_kernel,
+        out_shape=padded,
+        in_specs=[WHOLE] * 2,
+        out_specs=WHOLE,
+        compiler_params=params(16),
+        cost_estimate=cost(work, 4 * populations.size),
+        name="stream_own",
+    )(held(collided), held(field))
+    layer = near(45, height, length)
+    a_sent, b_sent = pl.pallas_call(
+        side_kernel,
+        out_shape=[layer, layer],
+        in_specs=[SCALARS, WHOLE, WHOLE, HBM, WHOLE, WHOLE],
+        out_specs=[WHOLE] * 2,
+        compiler_params=params(16),
+        name="side_layers",
+    )(parity, held(collided), held(field), streamed, held(low), held(high))
+    a_got = lax.ppermute(a_sent, "span", [(s, s ^ 1) for s in range(spans)])
+    b_got = lax.ppermute(
+        b_sent, "span", [(s, (s + 1 if s % 2 else s - 1) % spans) for s in range(spans)]
+    )
+    state, result, ring = pl.pallas_call(
         inner_kernel,
-        out_shape=[final, padded, padded, near(2, 9, 24, length)],
+        out_shape=[padded, padded, near(2, 9, 24, length)],
         in_specs=[SCALARS] + [WHOLE] * 6,
-        out_specs=[HBM] + [WHOLE] * 3,
-        scratch_shapes=[pltpu.SemaphoreType.DMA((SPLIT // 2,))],
+        out_specs=[WHOLE] * 3,
+        input_output_aliases={1: 0},
         compiler_params=params(16),
         cost_estimate=cost(work, 4 * populations.size),
         name="first_planes",
-    )(relax_rates, held(collided), held(field), *faces)
-    corner = near(15, 8, length)
-    halo, up_corner, down_corner = pl.pallas_call(
-        corner_kernel,
-        out_shape=[near(2, 30, height, length), corner, corner],
-        in_specs=[SCALARS] + [WHOLE] * 2 + [HBM],
-        out_specs=[WHOLE] * 3,
-        compiler_params=params(16),
-        name="corners",
-    )(parity, held(a_got), held(b_got), ring)
-    low_corner = lax.ppermute(up_corner, "leaf", upward)
-    high_corner = lax.ppermute(down_corner, "leaf", downward)
+    )(relax_rates, held(streamed), held(field), *faces)
     out, result = pl.pallas_call(
         more_kernel,
         out_shape=[final, padded],
-        in_specs=[SCALARS] + [WHOLE] * 4 + [HBM],
+        in_specs=[SCALARS] + [WHOLE] * 4,
         out_specs=[HBM, WHOLE],
-        input_output_aliases={4: 1, 5: 0},
+        input_output_aliases={4: 1},
         scratch_shapes=[pltpu.SemaphoreType.DMA((width // 2,))],
         compiler_params=params(16),
         cost_estimate=cost(work, 4 * populations.size),
         name="more_planes",
-    )(relax_rates, held(state), held(field), held(ring), held(result), far(out))
+    )(relax_rates, held(state), held(field), held(ring), held(result))
+    corner = near(15, 8, length)
+    halo, up_corner, down_corner, low_corner, high_corner = pl.pallas_call(
+        corner_kernel,
+        out_shape=[near(2, 45, height, length)] + [corner] * 4,
+        in_specs=[SCALARS] + [WHOLE] * 2 + [HBM],
+        out_specs=[WHOLE] * 5,
+        compiler_params=params(16),
+        name="corners",
+    )(parity, held(a_got), held(b_got), result)
     corners = [held(each) for each in (up_corner, down_corner, low_corner, high_corner)]
     return pl.pallas_call(
         outer_kernel,
@@ -617,10 +677,10 @@
         out_specs=[HBM, WHOLE, WHOLE],
         input_output_aliases={2: 1, 3: 2, 4: 0},
         scratch_shapes=[
-            pltpu.VMEM((2, 30, 24, length), F32),
-            pltpu.VMEM((2, 9, 24, length), F32),
-            pltpu.VMEM((2, 9, 24, length), F32),
-            pltpu.SemaphoreType.DMA((2,)),
+            pltpu.VMEM((2, 30, 8, length), F32),
+            pltpu.VMEM((2, 9, 8, length), F32),
+            pltpu.VMEM((2, 9, 8, length), F32),
+            pltpu.SemaphoreType.DMA((3,)),
         ],
         compiler_params=params(16),
         name="outer_planes",

time: 51.7 us -> 49.8 us (0.963)
  waiting for transfers between devices: 2.52 us -> 5.98 us
  starting transfers between devices: 31.6 us -> 28.4 us
  Pallas kernels: 14.6 us -> 12.9 us
    ppermute x6 -> x4, waiting for transfers between devices: 0.33 us -> 4.51 us  [the longest x1 2.77 us: body(): lax.ppermute(down, 'leaf', [(l, (l - 1) % leaves) for l in range(leaves)])]
    ppermute x6 -> x4, starting transfers between devices: 13.3 us -> 10 us  [the longest x1 6.18 us: body(): lax.ppermute(b_sent, 'span', [(s, (s + 1 if s % 2 else s - 1) % spans) fo...]
    pallas_call x3 -> x5, Pallas kernels: 6.22 us -> 5.49 us  [the longest x1 1.93 us: body(): pl.pallas_call(inner_kernel, out_shape=[padded, padded, near(2, 9, 24, le...]
    all_to_all x1, waiting for transfers between devices: 2.19 us -> 1.47 us  [body(): lax.all_to_all(sent, 'leaf', 0, 0, tiled=True, axis_index_groups=[group_o...]
  transfers between devices with their start and end apart: 7 -> 5, of which waited for: 2 -> 4; matrix products, arithmetic and copies ran while one was open for 0% -> 0% of each run, Pallas kernels for 16% -> 15%
where the time goes in v3:
time: 49.8 us; the launch traced here: 49.5 us
  starting transfers between devices  28.4 us (57%)
  Pallas kernels  12.9 us (26%)
  waiting for transfers between devices  5.98 us (12%)
  local copies, waits for them, and re-layouts  2.13 us (4%)
    all_to_all x1, starting transfers between devices, body(): lax.all_to_all(sent, 'leaf', 0, 0, tiled=True, axis_index_groups=[group_o...  18.3 us
    ppermute x1, starting transfers between devices, body(): lax.ppermute(b_sent, 'span', [(s, (s + 1 if s % 2 else s - 1) % spans) fo...  6.18 us
    ppermute x1, starting transfers between devices, body(): a_got = lax.ppermute(a_sent, 'span', [(s, s ^ 1) for s in range(spans)])  3.11 us
    ppermute x1, waiting for transfers between devices, body(): lax.ppermute(down, 'leaf', [(l, (l - 1) % leaves) for l in range(leaves)])  2.77 us
    unnamed x6, local copies, waits for them, and re-layouts  2.13 us
    pallas_call x1, Pallas kernels, body(): pl.pallas_call(more_kernel, out_shape=[final, padded], in_specs=[SCALARS]...  2.12 us
    pallas_call x1, Pallas kernels, body(): pl.pallas_call(inner_kernel, out_shape=[padded, padded, near(2, 9, 24, le...  1.93 us
    pallas_call x1, Pallas kernels, body(): pl.pallas_call(bin_kernel, out_shape=near(leaves, 1, 384), in_specs=[HBM]...  1.92 us
  transfers between devices with their start and end apart: 5, of which 4 were waited for; matrix products, arithmetic and copies ran while one was open for 0% of the time, Pallas kernels for 15%

profile of v3, /device:TPU:1, one launch (start us, length us, event | category | flops | bytes accessed | tf_op | source)
XLA Modules:
  0.0 49.5 jit_solution(10305120267255383574)
XLA Ops:
  0.0 1.9 %bin_markers.1.after_ref = f32[32,1,384]{2,1,0:T(1,128)} custom-call(f32[3,2,384]{2,1,0:T(2,128)} %bitcast.3, s32[2,1,384]{2,1,0:T(1,128)} %bitcast.4, s32[2,384]{1,0:T(2,128)} %cells_hbm.1), custom_call_target="tpu_custom_call" | custom-call | tf_op jit(solution)/shard_map/bin_markers/pallas_call | solution.py:568
  1.9 18.3 %all-to-all-start = ((f32[32,1,384]{2,1,0:T(1,128)}), f32[32,1,384]{2,1,0:T(1,128)S(1)}, u32[]{:S(2)}, u32[]{:S(2)}) async-start(f32[32,1,384]{2,1,0:T(1,128)} %bin_markers.1.after_ref), calls=%async_computation | async-start | bytes 98304 | tf_op jit(solution)/shard_map/all_to_all | solution.py:586
  20.3 0.0 copy-start
  20.3 1.5 %copy-done = f32[27,16,8,128]{3,2,1,0:T(8,128)S(1)} copy-done((f32[27,16,8,128]{3,2,1,0:T(8,128)S(1)}, f32[27,16,8,128]{3,2,1,0:T(8,128)}, u32[]{:S(2)}) %copy-start) | copy-done | bytes 1769496
  21.8 0.0 copy-start.1
  21.8 0.7 %copy-done.1 = f32[27]{0:T(128)S(1)} copy-done((f32[27]{0:T(128)S(1)}, f32[27]{0:T(128)}, u32[]{:S(2)}) %copy-start.1) | copy-done | bytes 132
  22.4 1.7 %collide_first.1.collided_ref = f32[27,16,8,128]{3,2,1,0:T(8,128)S(1)} custom-call(f32[27]{0:T(128)S(1)} %copy-done.1, f32[32,1,384]{2,1,0:T(1,128)} %bin_markers.1.after_ref, f32[27,16,8,128]{3,2,1,0:T(8,128)S(1)} %copy-done), custom_call_target="tpu_custom_call" | custom-call | flops 5308416 | bytes 3538944 | tf_op jit(solution)/shard_map/collide_first/pallas_call | solution.py:590
  24.1 1.5 %all-to-all-done.received_ref = f32[32,1,384]{2,1,0:T(1,128)S(1)} async-done(((f32[32,1,384]{2,1,0:T(1,128)}), f32[32,1,384]{2,1,0:T(1,128)S(1)}, u32[]{:S(2)}, u32[]{:S(2)}) %all-to-all-start) | async-done | bytes 49184 | tf_op jit(solution)/shard_map/all_to_all | solution.py:586
  25.6 1.9 %deposit.1 = (f32[2,3,16,8,128]{4,3,2,1,0:T(8,128)S(1)}, f32[30,16,128]{2,1,0:T(8,128)S(1)}, f32[30,16,128]{2,1,0:T(8,128)S(1)}) custom-call(f32[32,1,384]{2,1,0:T(1,128)S(1)} %all-to-all-done.received_ref, f32[27,16,8,128]{3,2,1,0:T(8,128)S(1)} %collide_first.1.collided_ref), custom_call_target="tpu_custom_call" | custom-call | tf_op jit(solution)/shard_map/deposit/pallas_call | solution.py:606
  27.5 0.7 %collective-permute-start = (f32[30,16,128]{2,1,0:T(8,128)S(1)}, f32[30,16,128]{2,1,0:T(8,128)S(1)}, u32[]{:S(2)}, u32[]{:S(2)}) collective-permute-start(f32[30,16,128]{2,1,0:T(8,128)S(1)} %get-tuple-element.22.up_ref), channel_id=1, source_target_pairs={{0,1},{1,2},{2,3},{3,4},{4,5},{5,6},{6,7},{7,8},{8,9},{9,10},{10,1... | collective-permute-start | bytes 737288 | tf_op jit(solution)/shard_map/ppermute | solution.py:614
  28.2 0.0 collective-permute-start.1
  28.2 1.5 %stream_own.1.after_ref.state_in = f32[27,20,8,128]{3,2,1,0:T(8,128)S(1)} custom-call(f32[27,16,8,128]{3,2,1,0:T(8,128)S(1)} %collide_first.1.collided_ref, f32[2,3,16,8,128]{4,3,2,1,0:T(8,128)S(1)} %get-tuple-element.21.field_ref), custom_call_target="tpu_custom_call" | custom-call | flops 5308416 | bytes 1769472 | tf_op jit(solution)/shard_map/stream_own/pallas_call | solution.py:620
  29.7 1.6 %collective-permute-done.low_ref = f32[30,16,128]{2,1,0:T(8,128)S(1)} collective-permute-done((f32[30,16,128]{2,1,0:T(8,128)S(1)}, f32[30,16,128]{2,1,0:T(8,128)S(1)}, u32[]{:S(2)}, u32[]{:S(2)}) %collective-permute-start) | collective-permute-done | bytes 245792 | tf_op jit(solution)/shard_map/ppermute | solution.py:614
  31.4 2.8 %collective-permute-done.1.high_ref = f32[30,16,128]{2,1,0:T(8,128)S(1)} collective-permute-done((f32[30,16,128]{2,1,0:T(8,128)S(1)}, f32[30,16,128]{2,1,0:T(8,128)S(1)}, u32[]{:S(2)}, u32[]{:S(2)}) %collective-permute-start.1) | collective-permute-done | bytes 245792 | tf_op jit(solution)/shard_map/ppermute | solution.py:615
  34.2 0.1 side_layers.1
  34.2 3.1 %collective-permute-start.2 = (f32[45,8,128]{2,1,0:T(8,128)S(1)}, f32[45,8,128]{2,1,0:T(8,128)S(1)}, u32[]{:S(2)}, u32[]{:S(2)}) collective-permute-start(f32[45,8,128]{2,1,0:T(8,128)S(1)} %get-tuple-element.24), channel_id=1, source_target_pairs={{0,32},{32,0},{64,96},{96,64},{128,160},{160,128},{192,224},{224,1... | collective-permute-start | bytes 552968 | tf_op jit(solution)/shard_map/ppermute | solution.py:638
  37.4 6.2 %collective-permute-start.3 = (f32[45,8,128]{2,1,0:T(8,128)S(1)}, f32[45,8,128]{2,1,0:T(8,128)S(1)}, u32[]{:S(2)}, u32[]{:S(2)}) collective-permute-start(f32[45,8,128]{2,1,0:T(8,128)S(1)} %get-tuple-element.25), channel_id=1, source_target_pairs={{0,480},{32,64},{64,32},{96,128},{128,96},{160,192},{192,160},{224... | collective-permute-start | bytes 552968 | tf_op jit(solution)/shard_map/ppermute | solution.py:639
  43.5 0.0 copy-done.2
  43.6 1.9 %first_planes.1 = (f32[27,20,8,128]{3,2,1,0:T(8,128)S(1)}, f32[27,20,8,128]{3,2,1,0:T(8,128)S(1)}, f32[2,9,24,128]{3,2,1,0:T(8,128)S(1)}) custom-call(f32[27]{0:T(128)S(1)} %copy-done.2, f32[27,20,8,128]{3,2,1,0:T(8,128)S(1)} %stream_own.1.after_ref.state_in, f32[2,3,16,8,128]{4,3,2,1,0:T(8,128)S(1)} %get-tuple-element.21.field_ref, ...), custom_call_target="tpu_custom_call", output_to_operand_aliasing={{0}: (1, {})} | custom-call | flops 5308416 | bytes 1769472 | tf_op jit(solution)/shard_map/first_planes/pallas_call | solution.py:642
  45.5 2.1 %more_planes.1 = (f32[27,16,8,128]{3,2,1,0:T(8,128)}, f32[27,20,8,128]{3,2,1,0:T(8,128)S(1)}) custom-call(f32[27]{0:T(128)S(1)} %copy-done.2, f32[27,20,8,128]{3,2,1,0:T(8,128)S(1)} %get-tuple-element.26.state.state_in, f32[2,3,16,8,128]{4,3,2,1,0:T(8,128)S(1)} %get-tuple-element.21.field_ref, ...), custom_call_target="tpu_custom_call", output_to_operand_aliasing={{1}: (4, {})} | custom-call | flops 5308416 | bytes 1769472 | tf_op jit(solution)/shard_map/more_planes/pallas_call | solution.py:652
  47.6 0.0 collective-permute-done.2.a_ref
  47.6 0.1 collective-permute-done.3.b_ref
  47.7 0.1 corners.1
  47.8 1.7 %outer_planes.1 = (f32[27,16,8,128]{3,2,1,0:T(8,128)}, f32[27,20,8,128]{3,2,1,0:T(8,128)S(1)}, f32[27,20,8,128]{3,2,1,0:T(8,128)S(1)}) custom-call(f32[27]{0:T(128)S(1)} %copy-done.2, f32[2,45,8,128]{3,2,1,0:T(8,128)S(1)} %get-tuple-element.30.halo_ref, ...), custom_call_target="tpu_custom_call", output_to_operand_aliasing={{1}: (2, {}), {2}: (3, {}), {0}: (4, {})} | custom-call | tf_op jit(solution)/shard_map/outer_planes/pallas_call | solution.py:673
  (1 shorter events, 0.0 us)
Async XLA Ops:
  1.9 23.6 %all-to-all-start = ((f32[32,1,384]{2,1,0:T(1,128)}), f32[32,1,384]{2,1,0:T(1,128)S(1)}, u32[]{:S(2)}, u32[]{:S(2)}) async-start(f32[32,1,384]{2,1,0:T(1,128)} %bin_markers.1.after_ref), calls=%async_computation | async-start | bytes 98304 | tf_op jit(solution)/shard_map/all_to_all | solution.py:586
  20.3 1.5 %copy-start = (f32[27,16,8,128]{3,2,1,0:T(8,128)S(1)}, f32[27,16,8,128]{3,2,1,0:T(8,128)}, u32[]{:S(2)}) copy-start(f32[27,16,8,128]{3,2,1,0:T(8,128)} %populations_ref.1) | copy-start | bytes 5308420
  21.8 0.7 %copy-start.1 = (f32[27]{0:T(128)S(1)}, f32[27]{0:T(128)}, u32[]{:S(2)}) copy-start(f32[27]{0:T(128)} %rates_ref.7) | copy-start | bytes 328
  27.5 3.9 %collective-permute-start = (f32[30,16,128]{2,1,0:T(8,128)S(1)}, f32[30,16,128]{2,1,0:T(8,128)S(1)}, u32[]{:S(2)}, u32[]{:S(2)}) collective-permute-start(f32[30,16,128]{2,1,0:T(8,128)S(1)} %get-tuple-element.22.up_ref), channel_id=1, source_target_pairs={{0,1},{1,2},{2,3},{3,4},{4,5},{5,6},{6,7},{7,8},{8,9},{9,10},{10,1... | collective-permute-start | bytes 737288 | tf_op jit(solution)/shard_map/ppermute | solution.py:614
  28.2 5.9 %collective-permute-start.1 = (f32[30,16,128]{2,1,0:T(8,128)S(1)}, f32[30,16,128]{2,1,0:T(8,128)S(1)}, u32[]{:S(2)}, u32[]{:S(2)}) collective-permute-start(f32[30,16,128]{2,1,0:T(8,128)S(1)} %get-tuple-element.23.down_ref), channel_id=1, source_target_pairs={{0,31},{1,0},{2,1},{3,2},{4,3},{5,4},{6,5},{7,6},{8,7},{9,8},{10,9... | collective-permute-start | bytes 737288 | tf_op jit(solution)/shard_map/ppermute | solution.py:615
  34.2 9.4 %copy-start.2 = (f32[27]{0:T(128)S(1)}, f32[27]{0:T(128)}, u32[]{:S(2)}) copy-start(f32[27]{0:T(128)} %rates_ref.7) | copy-start | bytes 328
  34.2 13.4 %collective-permute-start.2 = (f32[45,8,128]{2,1,0:T(8,128)S(1)}, f32[45,8,128]{2,1,0:T(8,128)S(1)}, u32[]{:S(2)}, u32[]{:S(2)}) collective-permute-start(f32[45,8,128]{2,1,0:T(8,128)S(1)} %get-tuple-element.24), channel_id=1, source_target_pairs={{0,32},{32,0},{64,96},{96,64},{128,160},{160,128},{192,224},{224,1... | collective-permute-start | bytes 552968 | tf_op jit(solution)/shard_map/ppermute | solution.py:638
  37.4 10.4 %collective-permute-start.3 = (f32[45,8,128]{2,1,0:T(8,128)S(1)}, f32[45,8,128]{2,1,0:T(8,128)S(1)}, u32[]{:S(2)}, u32[]{:S(2)}) collective-permute-start(f32[45,8,128]{2,1,0:T(8,128)S(1)} %get-tuple-element.25), channel_id=1, source_target_pairs={{0,480},{32,64},{64,32},{96,128},{128,96},{160,192},{192,160},{224... | collective-permute-start | bytes 552968 | tf_op jit(solution)/shard_map/ppermute | solution.py:639

commit v4 on v3

--- a/solution.py
+++ b/solution.py
@@ -184,7 +184,7 @@
             collided_ref[q, base + x] = result[q]
         return carry
 
-    lax.fori_loop(0, width, plane, 0)
+    lax.fori_loop(0, width, plane, 0, unroll=2)
 
 
 def rows_by_value(received_ref):
@@ -274,13 +274,17 @@
     return place // 2, pl.ds(4 * (place % 2) + number, 1)
 
 
+def layer_row(n, number, cz):
+    return 30 + n // 4, pl.ds(2 * (n % 4) + number - (1 - cz if cz >= 0 else 2), 1)
+
+
 def side_kernel(parity_ref, collided_ref, field_ref, after_ref, low_ref, high_ref, a_ref, b_ref):
     last = collided_ref.shape[1] - 1
 
     def layers(ref, sign, edge, inside):
-        def put(n, number, got, place, x):
-            tile, row = corner_at(n, number)
-            ref[30 + tile, row, :] = got[place, pl.ds(x, 1), :]
+        def put(n, number, cz, got, place, x):
+            tile, row = layer_row(n, number, cz)
+            ref[tile, row, :] = got[place, pl.ds(x, 1), :]
 
         for first, count, x in ((0, 18, edge), (18, 9, inside)):
             terms = sources([field_ref[0, c, x] for c in range(3)])
@@ -289,17 +293,17 @@
                 j, cz = q // 3, q % 3 - 1
                 ref[n] = pushed(collided_ref[q, x], terms[q])
                 if cz >= 0:
-                    put(n, 1, low_ref, 9 * cz + j, x)
+                    put(n, 1, cz, low_ref, 9 * cz + j, x)
                 if cz <= 0:
-                    put(n, 2, high_ref, -9 * cz + j, x)
+                    put(n, 2, cz, high_ref, -9 * cz + j, x)
                 if cz > 0:
-                    put(n, 0, low_ref, 18 + j, x)
+                    put(n, 0, cz, low_ref, 18 + j, x)
                 if cz < 0:
-                    put(n, 3, high_ref, 18 + j, x)
+                    put(n, 3, cz, high_ref, 18 + j, x)
         for c in range(3):
             ref[27 + c] = field_ref[1, c, edge]
-            put(27 + c, 1, low_ref, 27 + c, edge)
-            put(27 + c, 2, high_ref, 27 + c, edge)
+            put(27 + c, 1, 0, low_ref, 27 + c, edge)
+            put(27 + c, 2, 0, high_ref, 27 + c, edge)
 
     @pl.when(parity_ref[0] == 0)
     def _():
@@ -339,10 +343,10 @@
                 tile, row = corner_at(place, number)
                 ref[tile, row, :] = load(side, layer)
 
-    def outside(number):
+    def outside(number, cz):
         def load(side, layer):
-            tile, row = corner_at(layer, number)
-            return halo_ref[side, 30 + tile, row, :]
+            tile, row = layer_row(layer, number, cz)
+            return halo_ref[side, tile, row, :]
 
         return load
 
@@ -351,14 +355,14 @@
         (high_ref, up_ref, -1, 2, height - 1),
     ):
         for j in range(9):
-            columns(j, 0, outside(first), ref)
-            columns(9 + j, sign, outside(first), ref)
-            columns(18 + j, sign, outside(first - sign), ref)
+            columns(j, 0, outside(first, 0), ref)
+            columns(9 + j, sign, outside(first, sign), ref)
+            columns(18 + j, sign, outside(first - sign, sign), ref)
             columns(9 + j, -sign, lambda side, n: halo_ref[side, n, pl.ds(z, 1), :], own_ref)
         for c in range(3):
             for side, number in ((0, 1), (1, 2)):
                 tile, row = corner_at(27 + c, number)
-                ref[tile, row, :] = outside(first)(side, 27 + c)
+                ref[tile, row, :] = outside(first, 0)(side, 27 + c)
 
 
 def moved(tile, q, low_row, high_row):
@@ -414,7 +418,7 @@
         second(x + 2, [field_ref[1, c, x] for c in range(3)], rate, state, ring, result)
         return carry
 
-    lax.fori_loop(first, last, plane, 0)
+    lax.fori_loop(first, last, plane, 0, unroll=2)
 
 
 def stream_kernel(collided_ref, field_ref, state):
@@ -430,7 +434,7 @@
             state[q, x + 2 + cx] = tile
         return carry
 
-    lax.fori_loop(0, collided_ref.shape[1], own, 0)
+    lax.fori_loop(0, collided_ref.shape[1], own, 0, unroll=2)
 
 
 def inner_kernel(
@@ -460,7 +464,7 @@
                 ring[side, j, pl.ds(start + 2, 8), :] = rows[j]
             return carry
 
-        lax.fori_loop(0, 2, edge, 0)
+        lax.fori_loop(0, 2, edge, 0, unroll=2)
     planes(1, SPLIT, rate, field_ref, state, ring, result)
 
 
@@ -626,7 +630,7 @@
         cost_estimate=cost(work, 4 * populations.size),
         name="stream_own",
     )(held(collided), held(field))
-    layer = near(45, height, length)
+    layer = near(38, height, length)
     a_sent, b_sent = pl.pallas_call(
         side_kernel,
         out_shape=[layer, layer],
@@ -663,7 +667,7 @@
     corner = near(15, 8, length)
     halo, up_corner, down_corner, low_corner, high_corner = pl.pallas_call(
         corner_kernel,
-        out_shape=[near(2, 45, height, length)] + [corner] * 4,
+        out_shape=[near(2, 38, height, length)] + [corner] * 4,
         in_specs=[SCALARS] + [WHOLE] * 2 + [HBM],
         out_specs=[WHOLE] * 5,
         compiler_params=params(16),

time: 49.8 us -> 49.2 us (0.988)
  Pallas kernels: 12.9 us -> 11.3 us
  waiting for transfers between devices: 5.98 us -> 6.96 us
    pallas_call x1, Pallas kernels: 1.5 us -> 0.87 us  [body(): pl.pallas_call(stream_kernel, out_shape=padded, in_specs=[WHOLE] * 2, out...]
    ppermute x1, waiting for transfers between devices: 1.63 us -> 2.26 us  [body(): lax.ppermute(up, 'leaf', [(l, (l + 1) % leaves) for l in range(leaves)])]
    pallas_call x1, Pallas kernels: 1.93 us -> 1.38 us  [body(): pl.pallas_call(inner_kernel, out_shape=[padded, padded, near(2, 9, 24, le...]
  transfers between devices with their start and end apart: 5 -> 5, of which waited for: 4 -> 4; matrix products, arithmetic and copies ran while one was open for 0% -> 0% of each run, Pallas kernels for 15% -> 11%
where the time goes in v4:
time: 49.2 us; the launch traced here: 48.9 us
  starting transfers between devices  28.4 us (58%)
  Pallas kernels  11.3 us (23%)
  waiting for transfers between devices  6.96 us (14%)
  local copies, waits for them, and re-layouts  2.13 us (4%)
    all_to_all x1, starting transfers between devices, body(): lax.all_to_all(sent, 'leaf', 0, 0, tiled=True, axis_index_groups=[group_o...  18.3 us
    ppermute x1, starting transfers between devices, body(): lax.ppermute(b_sent, 'span', [(s, (s + 1 if s % 2 else s - 1) % spans) fo...  6.18 us
    ppermute x1, starting transfers between devices, body(): a_got = lax.ppermute(a_sent, 'span', [(s, s ^ 1) for s in range(spans)])  3.11 us
    ppermute x1, waiting for transfers between devices, body(): lax.ppermute(down, 'leaf', [(l, (l - 1) % leaves) for l in range(leaves)])  2.77 us
    ppermute x1, waiting for transfers between devices, body(): lax.ppermute(up, 'leaf', [(l, (l + 1) % leaves) for l in range(leaves)])  2.26 us
    unnamed x6, local copies, waits for them, and re-layouts  2.13 us
    pallas_call x1, Pallas kernels, body(): pl.pallas_call(bin_kernel, out_shape=near(leaves, 1, 384), in_specs=[HBM]...  1.92 us
    pallas_call x1, Pallas kernels, body(): pl.pallas_call(deposit_kernel, out_shape=[near(2, 3, width, height, lengt...  1.91 us
  transfers between devices with their start and end apart: 5, of which 4 were waited for; matrix products, arithmetic and copies ran while one was open for 0% of the time, Pallas kernels for 11%

profile of v4, /device:TPU:1, one launch (start us, length us, event | category | flops | bytes accessed | tf_op | source)
XLA Modules:
  0.0 48.9 jit_solution(8734068906140673204)
XLA Ops:
  0.0 1.9 %bin_markers.1.after_ref = f32[32,1,384]{2,1,0:T(1,128)} custom-call(f32[3,2,384]{2,1,0:T(2,128)} %bitcast.3, s32[2,1,384]{2,1,0:T(1,128)} %bitcast.4, s32[2,384]{1,0:T(2,128)} %cells_hbm.1), custom_call_target="tpu_custom_call" | custom-call | tf_op jit(solution)/shard_map/bin_markers/pallas_call | solution.py:572
  1.9 18.3 %all-to-all-start = ((f32[32,1,384]{2,1,0:T(1,128)}), f32[32,1,384]{2,1,0:T(1,128)S(1)}, u32[]{:S(2)}, u32[]{:S(2)}) async-start(f32[32,1,384]{2,1,0:T(1,128)} %bin_markers.1.after_ref), calls=%async_computation | async-start | bytes 98304 | tf_op jit(solution)/shard_map/all_to_all | solution.py:590
  20.3 0.0 copy-start
  20.3 1.5 %copy-done = f32[27,16,8,128]{3,2,1,0:T(8,128)S(1)} copy-done((f32[27,16,8,128]{3,2,1,0:T(8,128)S(1)}, f32[27,16,8,128]{3,2,1,0:T(8,128)}, u32[]{:S(2)}) %copy-start) | copy-done | bytes 1769496
  21.8 0.0 copy-start.1
  21.8 0.7 %copy-done.1 = f32[27]{0:T(128)S(1)} copy-done((f32[27]{0:T(128)S(1)}, f32[27]{0:T(128)}, u32[]{:S(2)}) %copy-start.1) | copy-done | bytes 132
  22.4 1.6 %collide_first.1.collided_ref = f32[27,16,8,128]{3,2,1,0:T(8,128)S(1)} custom-call(f32[27]{0:T(128)S(1)} %copy-done.1, f32[32,1,384]{2,1,0:T(1,128)} %bin_markers.1.after_ref, f32[27,16,8,128]{3,2,1,0:T(8,128)S(1)} %copy-done), custom_call_target="tpu_custom_call" | custom-call | flops 5308416 | bytes 3538944 | tf_op jit(solution)/shard_map/collide_first/pallas_call | solution.py:594
  24.0 1.5 %all-to-all-done.received_ref = f32[32,1,384]{2,1,0:T(1,128)S(1)} async-done(((f32[32,1,384]{2,1,0:T(1,128)}), f32[32,1,384]{2,1,0:T(1,128)S(1)}, u32[]{:S(2)}, u32[]{:S(2)}) %all-to-all-start) | async-done | bytes 49184 | tf_op jit(solution)/shard_map/all_to_all | solution.py:590
  25.6 1.9 %deposit.1 = (f32[2,3,16,8,128]{4,3,2,1,0:T(8,128)S(1)}, f32[30,16,128]{2,1,0:T(8,128)S(1)}, f32[30,16,128]{2,1,0:T(8,128)S(1)}) custom-call(f32[32,1,384]{2,1,0:T(1,128)S(1)} %all-to-all-done.received_ref, f32[27,16,8,128]{3,2,1,0:T(8,128)S(1)} %collide_first.1.collided_ref), custom_call_target="tpu_custom_call" | custom-call | tf_op jit(solution)/shard_map/deposit/pallas_call | solution.py:610
  27.5 0.7 %collective-permute-start = (f32[30,16,128]{2,1,0:T(8,128)S(1)}, f32[30,16,128]{2,1,0:T(8,128)S(1)}, u32[]{:S(2)}, u32[]{:S(2)}) collective-permute-start(f32[30,16,128]{2,1,0:T(8,128)S(1)} %get-tuple-element.22.up_ref), channel_id=1, source_target_pairs={{0,1},{1,2},{2,3},{3,4},{4,5},{5,6},{6,7},{7,8},{8,9},{9,10},{10,1... | collective-permute-start | bytes 737288 | tf_op jit(solution)/shard_map/ppermute | solution.py:618
  28.2 0.0 collective-permute-start.1
  28.2 0.9 %stream_own.1.after_ref.state_in = f32[27,20,8,128]{3,2,1,0:T(8,128)S(1)} custom-call(f32[27,16,8,128]{3,2,1,0:T(8,128)S(1)} %collide_first.1.collided_ref, f32[2,3,16,8,128]{4,3,2,1,0:T(8,128)S(1)} %get-tuple-element.21.field_ref), custom_call_target="tpu_custom_call" | custom-call | flops 5308416 | bytes 1769472 | tf_op jit(solution)/shard_map/stream_own/pallas_call | solution.py:624
  29.1 2.3 %collective-permute-done.low_ref = f32[30,16,128]{2,1,0:T(8,128)S(1)} collective-permute-done((f32[30,16,128]{2,1,0:T(8,128)S(1)}, f32[30,16,128]{2,1,0:T(8,128)S(1)}, u32[]{:S(2)}, u32[]{:S(2)}) %collective-permute-start) | collective-permute-done | bytes 245792 | tf_op jit(solution)/shard_map/ppermute | solution.py:618
  31.4 2.8 %collective-permute-done.1.high_ref = f32[30,16,128]{2,1,0:T(8,128)S(1)} collective-permute-done((f32[30,16,128]{2,1,0:T(8,128)S(1)}, f32[30,16,128]{2,1,0:T(8,128)S(1)}, u32[]{:S(2)}, u32[]{:S(2)}) %collective-permute-start.1) | collective-permute-done | bytes 245792 | tf_op jit(solution)/shard_map/ppermute | solution.py:619
  34.2 0.1 side_layers.1
  34.2 3.1 %collective-permute-start.2 = (f32[38,8,128]{2,1,0:T(8,128)S(1)}, f32[38,8,128]{2,1,0:T(8,128)S(1)}, u32[]{:S(2)}, u32[]{:S(2)}) collective-permute-start(f32[38,8,128]{2,1,0:T(8,128)S(1)} %get-tuple-element.24), channel_id=1, source_target_pairs={{0,32},{32,0},{64,96},{96,64},{128,160},{160,128},{192,224},{224,1... | collective-permute-start | bytes 466952 | tf_op jit(solution)/shard_map/ppermute | solution.py:642
  37.4 6.2 %collective-permute-start.3 = (f32[38,8,128]{2,1,0:T(8,128)S(1)}, f32[38,8,128]{2,1,0:T(8,128)S(1)}, u32[]{:S(2)}, u32[]{:S(2)}) collective-permute-start(f32[38,8,128]{2,1,0:T(8,128)S(1)} %get-tuple-element.25), channel_id=1, source_target_pairs={{0,480},{32,64},{64,32},{96,128},{128,96},{160,192},{192,160},{224... | collective-permute-start | bytes 466952 | tf_op jit(solution)/shard_map/ppermute | solution.py:643
  43.5 0.0 copy-done.2
  43.6 1.4 %first_planes.1 = (f32[27,20,8,128]{3,2,1,0:T(8,128)S(1)}, f32[27,20,8,128]{3,2,1,0:T(8,128)S(1)}, f32[2,9,24,128]{3,2,1,0:T(8,128)S(1)}) custom-call(f32[27]{0:T(128)S(1)} %copy-done.2, f32[27,20,8,128]{3,2,1,0:T(8,128)S(1)} %stream_own.1.after_ref.state_in, f32[2,3,16,8,128]{4,3,2,1,0:T(8,128)S(1)} %get-tuple-element.21.field_ref, ...), custom_call_target="tpu_custom_call", output_to_operand_aliasing={{0}: (1, {})} | custom-call | flops 5308416 | bytes 1769472 | tf_op jit(solution)/shard_map/first_planes/pallas_call | solution.py:646
  44.9 1.8 %more_planes.1 = (f32[27,16,8,128]{3,2,1,0:T(8,128)}, f32[27,20,8,128]{3,2,1,0:T(8,128)S(1)}) custom-call(f32[27]{0:T(128)S(1)} %copy-done.2, f32[27,20,8,128]{3,2,1,0:T(8,128)S(1)} %get-tuple-element.26.state.state_in, f32[2,3,16,8,128]{4,3,2,1,0:T(8,128)S(1)} %get-tuple-element.21.field_ref, ...), custom_call_target="tpu_custom_call", output_to_operand_aliasing={{1}: (4, {})} | custom-call | flops 5308416 | bytes 1769472 | tf_op jit(solution)/shard_map/more_planes/pallas_call | solution.py:656
  46.7 0.0 collective-permute-done.2.a_ref
  46.7 0.4 collective-permute-done.3.b_ref
  47.1 0.1 corners.1
  47.2 1.7 %outer_planes.1 = (f32[27,16,8,128]{3,2,1,0:T(8,128)}, f32[27,20,8,128]{3,2,1,0:T(8,128)S(1)}, f32[27,20,8,128]{3,2,1,0:T(8,128)S(1)}) custom-call(f32[27]{0:T(128)S(1)} %copy-done.2, f32[2,38,8,128]{3,2,1,0:T(8,128)S(1)} %get-tuple-element.30.halo_ref, ...), custom_call_target="tpu_custom_call", output_to_operand_aliasing={{1}: (2, {}), {2}: (3, {}), {0}: (4, {})} | custom-call | tf_op jit(solution)/shard_map/outer_planes/pallas_call | solution.py:677
  (1 shorter events, 0.0 us)
Async XLA Ops:
  1.9 23.6 %all-to-all-start = ((f32[32,1,384]{2,1,0:T(1,128)}), f32[32,1,384]{2,1,0:T(1,128)S(1)}, u32[]{:S(2)}, u32[]{:S(2)}) async-start(f32[32,1,384]{2,1,0:T(1,128)} %bin_markers.1.after_ref), calls=%async_computation | async-start | bytes 98304 | tf_op jit(solution)/shard_map/all_to_all | solution.py:590
  20.3 1.5 %copy-start = (f32[27,16,8,128]{3,2,1,0:T(8,128)S(1)}, f32[27,16,8,128]{3,2,1,0:T(8,128)}, u32[]{:S(2)}) copy-start(f32[27,16,8,128]{3,2,1,0:T(8,128)} %populations_ref.1) | copy-start | bytes 5308420
  21.8 0.7 %copy-start.1 = (f32[27]{0:T(128)S(1)}, f32[27]{0:T(128)}, u32[]{:S(2)}) copy-start(f32[27]{0:T(128)} %rates_ref.7) | copy-start | bytes 328
  27.5 3.9 %collective-permute-start = (f32[30,16,128]{2,1,0:T(8,128)S(1)}, f32[30,16,128]{2,1,0:T(8,128)S(1)}, u32[]{:S(2)}, u32[]{:S(2)}) collective-permute-start(f32[30,16,128]{2,1,0:T(8,128)S(1)} %get-tuple-element.22.up_ref), channel_id=1, source_target_pairs={{0,1},{1,2},{2,3},{3,4},{4,5},{5,6},{6,7},{7,8},{8,9},{9,10},{10,1... | collective-permute-start | bytes 737288 | tf_op jit(solution)/shard_map/ppermute | solution.py:618
  28.2 5.9 %collective-permute-start.1 = (f32[30,16,128]{2,1,0:T(8,128)S(1)}, f32[30,16,128]{2,1,0:T(8,128)S(1)}, u32[]{:S(2)}, u32[]{:S(2)}) collective-permute-start(f32[30,16,128]{2,1,0:T(8,128)S(1)} %get-tuple-element.23.down_ref), channel_id=1, source_target_pairs={{0,31},{1,0},{2,1},{3,2},{4,3},{5,4},{6,5},{7,6},{8,7},{9,8},{10,9... | collective-permute-start | bytes 737288 | tf_op jit(solution)/shard_map/ppermute | solution.py:619
  34.2 9.4 %copy-start.2 = (f32[27]{0:T(128)S(1)}, f32[27]{0:T(128)}, u32[]{:S(2)}) copy-start(f32[27]{0:T(128)} %rates_ref.7) | copy-start | bytes 328
  34.2 12.5 %collective-permute-start.2 = (f32[38,8,128]{2,1,0:T(8,128)S(1)}, f32[38,8,128]{2,1,0:T(8,128)S(1)}, u32[]{:S(2)}, u32[]{:S(2)}) collective-permute-start(f32[38,8,128]{2,1,0:T(8,128)S(1)} %get-tuple-element.24), channel_id=1, source_target_pairs={{0,32},{32,0},{64,96},{96,64},{128,160},{160,128},{192,224},{224,1... | collective-permute-start | bytes 466952 | tf_op jit(solution)/shard_map/ppermute | solution.py:642
  37.4 9.8 %collective-permute-start.3 = (f32[38,8,128]{2,1,0:T(8,128)S(1)}, f32[38,8,128]{2,1,0:T(8,128)S(1)}, u32[]{:S(2)}, u32[]{:S(2)}) collective-permute-start(f32[38,8,128]{2,1,0:T(8,128)S(1)} %get-tuple-element.25), channel_id=1, source_target_pairs={{0,480},{32,64},{64,32},{96,128},{128,96},{160,192},{192,160},{224... | collective-permute-start | bytes 466952 | tf_op jit(solution)/shard_map/ppermute | solution.py:643
